TPU v7x, 32 devices: a whole 2x2x4 slice. The times are simulated.
32 devices in a mesh: req: 4 (over x, core), gx: 4 (over z), gy: 2 (over y).
Axes of the slice: x: 2, y: 2, z: 4, core: 2. Of those that a mesh axis runs over, the one named last changes fastest.
Arguments:
- hidden: bfloat16 [3072, 4096], P(('req', 'gx'), 'gy')
- ln_gain: float32 [4096], P('gy'), may hold values from 0.25 to 1.75
- w_qkv: bfloat16 [4096, 32, 384], P('gy', 'gx'), may hold values from -0.09375 to 0.09375
- w_out: bfloat16 [4096, 4096], P('gx', 'gy'), may hold values from -0.375 to 0.375
- kv_cache: bfloat16 [8, 2176, 2, 4096], P('req', 'gy', None, 'gx')
- cache_len: int32 [8], P('req'), may hold values from 0 to 1792, as said below
Outputs:
- mixed: bfloat16 [3072, 4096], P(('req', 'gx'), 'gy')
- cache_out: bfloat16 [8, 2176, 2, 4096], P('req', 'gy', None, 'gx')
Inputs may be any that keep to these rules, and one draw needn't show every extreme that they name: `cache_len`: cached lengths are heavy-tailed; some request has exactly 1792.
All inputs are finite; a program needn't handle non-finite values.
Results may differ from a plain program's by a relative error of at most 0.04.
Values may be sent and summed in bfloat16 or wider, within the bound.
A program may use at most 128 MiB of HBM per device.

v0:
```python
import math

import jax
import jax.numpy as jnp
from jax import lax
from jax.sharding import PartitionSpec as P

D = 4096


norm_eps = 1e-05
floor_score = -1e30


def partial_attend(query, keys, values, valid, distance, slopes, scale):
    scores = jnp.einsum("chd,phd->chp", query, keys, preferred_element_type=jnp.float32) * scale
    scores = scores - slopes[None, :, None] * distance.astype(jnp.float32)[:, None, :]
    scores = jnp.where(valid[:, None, :], scores, floor_score)
    highest = jnp.max(scores, axis=-1)
    weights = jnp.where(valid[:, None, :], jnp.exp(scores - highest[..., None]), 0.0)
    totals = jnp.sum(weights, axis=-1)
    accum = jnp.einsum(
        "chp,phd->chd", weights.astype(jnp.bfloat16), values, preferred_element_type=jnp.float32
    )
    return (highest, totals, accum)


def write_cache(fresh_rows, cache_block, positions, length, group):
    offset = positions - length
    inside = (offset >= 0) & (offset < group)
    taken = jnp.take(fresh_rows, jnp.clip(offset, 0, group - 1), axis=0)
    return jnp.where(inside[:, None, None], taken, cache_block)


def shards(hidden, ln_gain, w_qkv, w_out, kv_cache, cache_len):
    hidden_f = hidden.astype(jnp.float32)
    sums = lax.psum((jnp.sum(hidden_f, axis=1), jnp.sum(hidden_f * hidden_f, axis=1)), "gy")
    mean = sums[0] / D
    var = sums[1] / D - mean * mean
    normed = (
        (hidden_f - mean[:, None]) * lax.rsqrt(var + norm_eps)[:, None] * ln_gain[None, :]
    ).astype(jnp.bfloat16)
    local_heads = w_qkv.shape[1]
    head_size = w_qkv.shape[2] // 3
    weight_flat = w_qkv.reshape(w_qkv.shape[0], local_heads * 3 * head_size)
    partial_value = jnp.dot(
        lax.all_gather(normed, "gx", axis=0, tiled=True),
        weight_flat,
        preferred_element_type=jnp.float32,
    )
    requests = cache_len.shape[0]
    all_rows = partial_value.shape[0]
    group = all_rows // requests
    width_local = local_heads * head_size
    block = kv_cache.shape[1]
    positions = lax.axis_index("gy") * block + jnp.arange(block, dtype=jnp.int32)
    head_ids = lax.axis_index("gx") * local_heads + jnp.arange(local_heads, dtype=jnp.int32)
    all_heads = local_heads * lax.axis_size("gx")
    slopes = jnp.exp2(-8.0 * (head_ids + 1).astype(jnp.float32) / all_heads)
    scale = 1.0 / math.sqrt(head_size)
    steps_c = jnp.arange(group, dtype=jnp.int32)
    tops_list = []
    totals_list = []
    accum_list = []
    caches = []
    qkv = lax.psum(partial_value.astype(jnp.bfloat16), "gy")
    qkv = qkv.reshape(requests, group, local_heads, 3 * head_size)
    fresh = jnp.stack(
        [
            qkv[:, :, :, head_size : 2 * head_size].reshape(requests, group, width_local),
            qkv[:, :, :, 2 * head_size :].reshape(requests, group, width_local),
        ],
        axis=2,
    )
    for request in range(requests):
        length = cache_len[request]
        updated = write_cache(fresh[request], kv_cache[request], positions, length, group)
        caches.append(updated)
        keys = updated[:, 0].reshape(block, local_heads, head_size)
        values = updated[:, 1].reshape(block, local_heads, head_size)
        distance = (length + steps_c)[:, None] - positions[None, :]
        part_top, part_total, part_accum = partial_attend(
            qkv[request, :, :, :head_size], keys, values, distance >= 0, distance, slopes, scale
        )
        tops_list.append(part_top)
        totals_list.append(part_total)
        accum_list.append(part_accum)
    tops = jnp.stack(tops_list)
    totals = jnp.stack(totals_list)
    accums = jnp.stack(accum_list)
    overall = lax.pmax(tops, "gy")
    factor = jnp.exp(tops - overall)
    joined_totals, joined_accums = (
        lax.psum((totals * factor).astype(jnp.bfloat16), "gy").astype(jnp.float32),
        lax.psum((accums * factor[..., None]).astype(jnp.bfloat16), "gy").astype(jnp.float32),
    )
    attn = (
        (joined_accums / joined_totals[..., None])
        .astype(jnp.bfloat16)
        .reshape(requests * group, width_local)
    )
    projected = lax.psum_scatter(
        jnp.dot(attn, w_out, preferred_element_type=jnp.float32).astype(jnp.bfloat16),
        "gx",
        scatter_dimension=0,
        tiled=True,
    ).astype(jnp.float32)
    mixed = (projected + hidden_f).astype(jnp.bfloat16)
    return (mixed, jnp.stack(caches))


def solution(mesh):
    in_specs = (
        P(("req", "gx"), "gy"),
        P("gy"),
        P("gy", "gx", None),
        P("gx", "gy"),
        P("req", "gy", None, "gx"),
        P("req"),
    )
    out_specs = (P(("req", "gx"), "gy"), P("req", "gy", None, "gx"))
    return jax.shard_map(shards, mesh=mesh, in_specs=in_specs, out_specs=out_specs, check_vma=False)
```

profile of v0, /device:TPU:0, one launch (start us, length us, event | category | flops | bytes accessed | tf_op | source)
XLA Modules:
  0.0 559.4 jit_solution(18295832827911686435)
XLA Ops:
  7.2 0.0 all-gather.2.cloned.1.call-start
  7.2 1.5 convert_reduce_fusion
  8.7 5.9 %all-reduce = (f32[192]{0:T(256)S(1)}, f32[192]{0:T(256)S(1)}) all-reduce(f32[192]{0:T(256)S(1)} %get-tuple-element.10, f32[192]{0:T(256)S(1)} %get-tuple-element.9), channel_id=1, replica_groups=mesh['req'=4,'gx'=4,'gy'=2] {'gy'}, use_global_device_ids=true, to_apply=%region_3.0 | all-reduce | flops 384 | bytes 3072 | tf_op jit(solution)/shard_map/psum | solution.py:37
  14.6 2.5 fusion.28
  17.1 0.0 all-gather.2.cloned.1.call-update
  17.1 0.0 all-reduce.4.cloned.1.call-start
  17.1 12.1 %copy.38 = bf16[256,8,8,384]{3,1,2,0:T(8,128)(2,1)} copy(bf16[256,8,8,384]{3,2,1,0:T(8,128)(2,1)} %bitcast.96) | data formatting | bytes 25165824
  29.2 53.3 %all-gather.2.cloned.1.call-done = bf16[768,2048]{1,0:T(8,128)(2,1)} async-done(((bf16[192,2048]{1,0:T(8,128)(2,1)}), bf16[768,2048]{1,0:T(8,128)(2,1)}) %all-gather.2.cloned.1.call-update) | async-done | bytes 3145744 | tf_op jit(solution)/shard_map/all_gather | solution.py:47
  82.5 13.8 %convolution_convert_fusion = bf16[768,3072]{1,0:T(8,128)(2,1)S(1)} fusion(bf16[768,2048]{1,0:T(8,128)(2,1)} %all-gather.2.cloned.1.call-done, bf16[2048,3072]{1,0:T(8,128)(2,1)} %bitcast.97), kind=kOutput, calls=%fused_computation.25 | convolution fusion | flops 9666035712 | bytes 20447232 | tf_op jit(solution)/shard_map/dot_general | solution.py:46
  96.3 1.2 copy.39
  97.5 3.0 copy.24
  100.5 0.0 copy-start.6
  100.5 0.0 all-reduce.4.cloned.1.call-update
  100.5 0.3 all-reduce.6.cloned.1.call-start
  100.8 0.3 copy-done.6
  101.1 0.6 fusion.50
  101.7 1.2 compare_and_fusion
  102.9 1.2 compare_and_fusion.2
  104.1 1.2 iota_add_fusion.1
  105.3 1.2 compare_select_fusion
  106.6 1.5 subtract_compare_fusion.1
  108.1 2.0 subtract_convert_fusion.1
  110.1 108.4 %all-reduce.4.cloned.1.call-done = bf16[2,384,8,384]{3,1,2,0:T(8,128)(2,1)} async-done(((bf16[2,384,8,384]{3,1,2,0:T(8,128)(2,1)}), bf16[2,384,8,384]{3,1,2,0:T(8,128)(2,1)}) %all-reduce.4.cloned.1.call-update) | async-done | bytes 4718608 | tf_op jit(solution)/shard_map/psum | solution.py:66
  218.5 2.1 fusion.49
  220.6 1.6 copy.25
  222.2 8.4 %copy.27 = bf16[2,384,1,1024]{3,2,1,0:T(2,128)(2,1)} copy(bf16[2,384,1,1024]{1,3,0,2:T(8,128)(2,1)} %bitcast.98) | data formatting | bytes 3145728 | tf_op jit(solution)/shard_map/stack;reshape | solution.py:68
  230.6 0.9 copy.26
  231.5 5.6 %copy.28 = bf16[2,384,1,1024]{3,2,1,0:T(2,128)(2,1)} copy(bf16[2,384,1,1024]{1,3,0,2:T(8,128)(2,1)S(1)} %bitcast.99) | data formatting | bytes 3145728 | tf_op jit(solution)/shard_map/stack;reshape | solution.py:68
  237.1 8.1 %fusion.34 = (bf16[384,2,1024]{2,1,0:T(2,128)(2,1)S(1)}, bf16[384,2,1024]{2,1,0:T(2,128)(2,1)S(1)}) fusion(bf16[2,384,1,1024]{3,2,1,0:T(2,128)(2,1)} %copy.28, bf16[2,384,1,1024]{3,2,1,0:T(2,128)(2,1)} %copy.27), kind=kLoop, calls=%fused_computation.62 | loop fusion | flops 6291456 | bytes 6291456 | tf_op jit(solution)/shard_map/squeeze | solution.py:77
  245.2 34.9 %gather_fusion = bf16[1088,2,1024]{2,1,0:T(2,128)(2,1)} fusion(bf16[384,2,1024]{2,1,0:T(2,128)(2,1)S(1)} %get-tuple-element.17, s32[2048]{0:T(1024)S(1)} %pad_clamp_fusion.1), kind=kCustom, calls=%fused_computation.clone | custom fusion | bytes 8917248 | tf_op jit(solution)/shard_map/jit(_take)/gather | solution.py:31
  280.1 35.0 %gather_fusion.1 = bf16[1088,2,1024]{2,1,0:T(2,128)(2,1)} fusion(bf16[384,2,1024]{2,1,0:T(2,128)(2,1)S(1)} %get-tuple-element.18, s32[2048]{0:T(1024)S(1)} %pad_clamp_fusion), kind=kCustom, calls=%fused_computation.1.clone | custom fusion | bytes 8917248 | tf_op jit(solution)/shard_map/jit(_take)/gather | solution.py:31
  315.1 19.8 %broadcast_select_fusion.1 = (bf16[1088,2,1024]{2,1,0:T(2,128)(2,1)S(1)}, bf16[1088,2,1024]{2,1,0:T(2,128)(2,1)}) fusion(pred[1088]{0:T(1024)(128)(4,1)S(1)} %get-tuple-element.38, bf16[1088,2,1024]{2,1,0:T(2,128)(2,1)} %gather_fusion, pred[1088]{0:T(1024)(128)(4,1)S(1)} %get-tuple-element.36, bf16[2,1088,2,1024]{3,2,1,0:T(2,128)(2,1)} %param.12, ...), kind=kLoop, calls=%fused_computation.14 | loop fusion | flops 8912896 | bytes 26743040 | tf_op jit(solution)/shard_map/jit(_where)/select_n | solution.py:32
  334.9 0.0 copy-start
  334.9 26.2 %slice_reduce_fusion.3 = (bf16[1088,1024]{1,0:T(8,128)(2,1)}, bf16[1088,1024]{1,0:T(8,128)(2,1)}) fusion(bf16[1088,2,1024]{2,1,0:T(2,128)(2,1)S(1)} %get-tuple-element.15), kind=kLoop, calls=%fused_computation.29 | loop fusion | bytes 8912896 | tf_op jit(solution)/shard_map/slice | solution.py:80
  361.1 0.0 copy-done
  361.1 29.5 %slice_reduce_fusion.1 = (bf16[1088,1024]{1,0:T(8,128)(2,1)}, bf16[1088,1024]{1,0:T(8,128)(2,1)}) fusion(bf16[1088,2,1024]{2,1,0:T(2,128)(2,1)} %get-tuple-element.16), kind=kLoop, calls=%fused_computation.27 | loop fusion | bytes 8912896 | tf_op jit(solution)/shard_map/slice | solution.py:80
  390.7 0.0 copy-done.5
  390.7 5.3 fusion.51
  396.0 2.3 fusion.4
  398.3 0.0 copy-start.2
  398.3 0.0 copy-start.3
  398.3 0.0 copy-start.4
  398.3 5.7 %fusion.40 = f32[1,384,8,128]{1,3,2,0:T(8,128)} fusion(f32[384,8,1088]{0,2,1:T(8,128)S(1)} %get-tuple-element.30, f32[384,8]{0,1:T(8,128)S(1)} %get-tuple-element.29, pred[384,1088]{0,1:T(8,128)(4,1)S(1)} %copy-done.5, bf16[1088,1024]{1,0:T(8,128)(2,1)} %get-tuple-element.7), kind=kOutput, calls=%fused_computation.64 | convolution fusion | flops 865665024 | bytes 17600512 | tf_op jit(solution)/shard_map/chp,phd->chd/dot_general | solution.py:22
  404.0 0.0 copy-done.2
  404.0 0.0 copy-done.3
  404.0 0.0 copy-done.4
  404.0 4.8 fusion.52
  408.8 2.3 fusion.2
  411.1 5.8 %fusion.35 = f32[1,384,8,128]{1,3,2,0:T(8,128)} fusion(f32[384,8,1088]{0,2,1:T(8,128)S(1)} %get-tuple-element.32, f32[384,8]{0,1:T(8,128)S(1)} %get-tuple-element.31, pred[384,1088]{0,1:T(8,128)(4,1)S(1)} %copy-done.4, bf16[1088,1024]{1,0:T(8,128)(2,1)} %get-tuple-element.5), kind=kOutput, calls=%fused_computation.63 | convolution fusion | flops 865665024 | bytes 17600512 | tf_op jit(solution)/shard_map/chp,phd->chd/dot_general | solution.py:22
  416.9 6.8 %pmax.7 = f32[2,384,8]{1,2,0:T(8,128)S(1)} all-reduce(f32[2,384,8]{1,2,0:T(8,128)S(1)} %pad_maximum_fusion.2), channel_id=1, replica_groups=mesh['req'=4,'gx'=4,'gy'=2] {'gy'}, use_global_device_ids=true, to_apply=%region_7.9 | all-reduce | flops 6144 | bytes 49152 | tf_op jit(solution)/shard_map/pmax | solution.py:91
  423.8 3.4 fusion.16
  427.1 0.0 all-reduce.6.cloned.1.call-update
  427.2 0.0 reduce-scatter.2.cloned.1.call-start
  427.2 8.6 %psum.39 = bf16[2,384,8]{1,2,0:T(8,128)(2,1)S(1)} all-reduce(bf16[2,384,8]{1,2,0:T(8,128)(2,1)S(1)} %get-tuple-element.13), channel_id=1, replica_groups=mesh['req'=4,'gx'=4,'gy'=2] {'gy'}, use_global_device_ids=true, to_apply=%region_11.13 | all-reduce | flops 6144 | bytes 24576 | tf_op jit(solution)/shard_map/psum | solution.py:94
  435.8 44.2 %all-reduce.6.cloned.1.call-done = bf16[2,384,8,128]{1,3,2,0:T(8,128)(2,1)} async-done(((bf16[2,384,8,128]{1,3,2,0:T(8,128)(2,1)}), bf16[2,384,8,128]{1,3,2,0:T(8,128)(2,1)}) %all-reduce.6.cloned.1.call-update) | async-done | bytes 1572880 | tf_op jit(solution)/shard_map/psum | solution.py:95
  480.0 1.7 divide_convert_fusion
  481.7 1.2 copy.33
  483.0 7.0 %convolution_convert_fusion.1 = bf16[768,2048]{1,0:T(8,128)(2,1)} fusion(bf16[1024,2048]{1,0:T(8,128)(2,1)} %param.11, bf16[96,8,8,128]{3,2,1,0:T(8,128)(2,1)S(1)} %bitcast.101), kind=kOutput, calls=%fused_computation.30 | convolution fusion | flops 3222798336 | bytes 8912896 | tf_op jit(solution)/shard_map/dot_general | solution.py:103
  489.9 0.0 reduce-scatter.2.cloned.1.call-update
  490.0 0.0 copy-start.1
  490.0 15.7 %pad_maximum_fusion = bf16[2,1088,2,1024]{3,2,1,0:T(2,128)(2,1)} fusion(bf16[1,1088,2,1024]{3,2,1,0:T(2,128)(2,1)} %bitcast.94, bf16[1,1088,2,1024]{3,2,1,0:T(2,128)(2,1)} %bitcast.93), kind=kLoop, calls=%fused_computation.12 | loop fusion | flops 4456448 | bytes 17825792 | tf_op jit(solution)/shard_map/stack | solution.py:109
  505.6 44.7 %reduce-scatter.2.cloned.1.call-done = bf16[192,2048]{1,0:T(8,128)(2,1)} async-done(((bf16[768,2048]{1,0:T(8,128)(2,1)}), bf16[192,2048]{1,0:T(8,128)(2,1)}) %reduce-scatter.2.cloned.1.call-update) | async-done | bytes 786448 | tf_op jit(solution)/shard_map/reduce_scatter | solution.py:102
  550.4 0.0 copy-done.1
  550.4 2.3 fusion.30
  (9 shorter events, 0.1 us)
Async XLA Ops:
  7.2 75.4 %all-gather.2.cloned.1.call-start = ((), (), s32[]{:S(2)}) async-start(), calls=%async_computation.1 | async-start | bytes 3932160 | tf_op jit(solution)/shard_map/all_gather | solution.py:47
  17.1 201.5 %all-reduce.4.cloned.1.call-start = ((), (), s32[]{:S(2)}) async-start(), calls=%async_computation.2 | async-start | bytes 9437184 | tf_op jit(solution)/shard_map/psum | solution.py:66
  100.5 0.7 copy-start.6
  100.5 379.5 %all-reduce.6.cloned.1.call-start = ((), (), s32[]{:S(2)}) async-start(), calls=%async_computation.3 | async-start | bytes 3145728 | tf_op jit(solution)/shard_map/psum | solution.py:95
  334.9 26.3 %copy-start = (bf16[1088,2,1024]{2,1,0:T(2,128)(2,1)}, bf16[1088,2,1024]{2,1,0:T(2,128)(2,1)S(1)}, u32[]{:S(2)}) copy-start(bf16[1088,2,1024]{2,1,0:T(2,128)(2,1)S(1)} %get-tuple-element.15) | copy-start | bytes 13369348
  361.1 29.5 %copy-start.5 = (pred[384,1088]{0,1:T(8,128)(4,1)S(1)}, pred[384,1088]{0,1:T(8,128)(4,1)}, u32[]{:S(2)}) copy-start(pred[384,1088]{0,1:T(8,128)(4,1)} %get-tuple-element.22) | copy-start | bytes 1253380
  398.3 5.7 %copy-start.2 = (bf16[1088,1024]{1,0:T(8,128)(2,1)S(1)}, bf16[1088,1024]{1,0:T(8,128)(2,1)}, u32[]{:S(2)}) copy-start(bf16[1088,1024]{1,0:T(8,128)(2,1)} %get-tuple-element.6) | copy-start | bytes 6684676
  398.3 5.7 %copy-start.3 = (f32[384,1088]{0,1:T(8,128)S(1)}, f32[384,1088]{0,1:T(8,128)}, u32[]{:S(2)}) copy-start(f32[384,1088]{0,1:T(8,128)} %get-tuple-element.23) | copy-start | bytes 5013508
  398.3 5.7 %copy-start.4 = (pred[384,1088]{0,1:T(8,128)(4,1)S(1)}, pred[384,1088]{0,1:T(8,128)(4,1)}, u32[]{:S(2)}) copy-start(pred[384,1088]{0,1:T(8,128)(4,1)} %get-tuple-element.21) | copy-start | bytes 1253380
  427.2 123.2 %reduce-scatter.2.cloned.1.call-start = ((), (), s32[]{:S(2)}) async-start(), calls=%async_computation.4 | async-start | bytes 3932160 | tf_op jit(solution)/shard_map/reduce_scatter | solution.py:102
  490.0 60.4 %copy-start.1 = (bf16[192,2048]{1,0:T(8,128)(2,1)S(1)}, bf16[192,2048]{1,0:T(8,128)(2,1)}, u32[]{:S(2)}) copy-start(bf16[192,2048]{1,0:T(8,128)(2,1)} %param.8) | copy-start | bytes 2359300
Sparse Core Ops, SparseCore 0:
  17.2 65.2 all-gather.1
  100.6 117.8 all-reduce.3
  427.3 52.6 all-reduce.5
  490.1 60.2 reduce-scatter.1
where the time goes:
time: 565 us; the launch traced here: 559 us
  waiting for transfers between devices  251 us (44%)
  local copies, waits for them, and re-layouts  163 us (29%)
  other arithmetic  67.9 us (12%)
  matrix products  42.3 us (7%)
  blocking collectives  21.3 us (4%)
  between operations  14.2 us (3%)
    psum x1, waiting for transfers between devices, shards(): qkv = lax.psum(partial_value.astype(jnp.bfloat16), 'gy')  108 us
    gather x2, local copies, waits for them, and re-layouts, write_cache(): taken = jnp.take(fresh_rows, jnp.clip(offset, 0, group - 1), axis=0)  69.9 us
    slice x2, local copies, waits for them, and re-layouts, shards(): values = updated[:, 1].reshape(block, local_heads, head_size)  55.8 us
    all_gather x1, waiting for transfers between devices, shards(): lax.all_gather(normed, 'gx', axis=0, tiled=True)  53.3 us
    reduce_scatter x1, waiting for transfers between devices, shards(): lax.psum_scatter(jnp.dot(attn, w_out, preferred_element_type=jnp.float32)...  44.7 us
    psum x1, waiting for transfers between devices, shards(): lax.psum((accums * factor[..., None]).astype(jnp.bfloat16), 'gy')  44.2 us
    select_n x1, other arithmetic, write_cache(): return jnp.where(inside[:, None, None], taken, cache_block)  19.8 us
    another operation x1, other arithmetic, shards(): return (mixed, jnp.stack(caches))  15.7 us
  transfers between devices with their start and end apart: 4, of which 4 were waited for; matrix products, arithmetic and copies ran while one was open for 7% of the time, Pallas kernels for 0%

commit v1 on v0

v1 whole, which is shorter than its diff:
```python
import math

import jax
import jax.numpy as jnp
from jax import lax
from jax.sharding import PartitionSpec as P

D = 4096
CHUNKS = 1

norm_eps = 1e-05
floor_score = -1e30


def other(value):
    return lax.ppermute(value, "gy", [(0, 1), (1, 0)])


def sum_gy(value):
    if lax.axis_size("gy") == 2:
        total = value.astype(jnp.float32) + other(value).astype(jnp.float32)
        return total.astype(value.dtype)
    return lax.psum(value, "gy")


def scatter_gy(value):
    n = lax.axis_size("gy")
    if n == 2:
        half = value.shape[1] // 2
        me = lax.axis_index("gy")
        low, high = value[:, :half], value[:, half:]
        first = me == 0
        arrived = other(jnp.where(first, high, low)).astype(jnp.float32)
        own = jnp.where(first, low, high).astype(jnp.float32)
        return (own + arrived).astype(value.dtype)
    return lax.psum_scatter(value, "gy", scatter_dimension=1, tiled=True)


def combine(top, total, accum):
    if lax.axis_size("gy") == 2:
        safe = jnp.where(total > 0, total, 1.0)
        part = (accum / safe[..., None]).astype(jnp.bfloat16)
        stats = jnp.stack([top, total])
        far_stats = other(stats)
        far_part = other(part)
        overall = jnp.maximum(top, far_stats[0])
        mine = jnp.exp(top - overall) * total
        far = jnp.exp(far_stats[0] - overall) * far_stats[1]
        joined = mine + far
        return (
            part.astype(jnp.float32) * (mine / joined)[..., None]
            + far_part.astype(jnp.float32) * (far / joined)[..., None]
        ).astype(jnp.bfloat16)
    factor = jnp.exp(top - lax.pmax(top, "gy"))
    totals = lax.psum(total * factor, "gy")
    accums = lax.psum((accum * factor[..., None]).astype(jnp.bfloat16), "gy")
    return (accums.astype(jnp.float32) / totals[..., None]).astype(jnp.bfloat16)


def split_cache(cache):
    requests, block, _, width = cache.shape
    size = math.gcd(2 * block, 128)
    rows = cache.reshape(requests, 2 * block // size, size, width)
    target = jnp.arange(size)[:, None]
    source = jnp.arange(size)[None, :]
    half = size // 2
    pick = (source == 2 * (target % half) + target // half).astype(cache.dtype)
    ordered = jnp.einsum("ks,rbsd->rbkd", pick, rows, preferred_element_type=jnp.float32)
    ordered = ordered.astype(cache.dtype)
    return (
        ordered[:, :, :half].reshape(requests, block, width),
        ordered[:, :, half:].reshape(requests, block, width),
    )


def partial_attend(query, keys, values, valid, distance, slopes, scale):
    scores = jnp.einsum("chd,phd->chp", query, keys, preferred_element_type=jnp.float32) * scale
    scores = scores - slopes[None, :, None] * distance.astype(jnp.float32)[:, None, :]
    scores = jnp.where(valid[:, None, :], scores, floor_score)
    highest = jnp.max(scores, axis=-1)
    weights = jnp.where(valid[:, None, :], jnp.exp(scores - highest[..., None]), 0.0)
    totals = jnp.sum(weights, axis=-1)
    accum = jnp.einsum(
        "chp,phd->chd", weights.astype(jnp.bfloat16), values, preferred_element_type=jnp.float32
    )
    return (highest, totals, accum)


def shards(hidden, ln_gain, w_qkv, w_out, kv_cache, cache_len):
    local_rows = hidden.shape[0]
    gx_n = lax.axis_size("gx")
    gy_n = lax.axis_size("gy")
    gy = lax.axis_index("gy")
    hidden_f = hidden.astype(jnp.float32)
    piece = local_rows // CHUNKS
    gathered = [
        lax.all_gather(hidden[c * piece : (c + 1) * piece], "gx", axis=0) for c in range(CHUNKS)
    ]
    sums = sum_gy(jnp.stack([jnp.sum(hidden_f, axis=1), jnp.sum(hidden_f * hidden_f, axis=1)]))
    mean = sums[0] / D
    rstd = lax.rsqrt(sums[1] / D - mean * mean + norm_eps)
    stats = lax.all_gather(jnp.stack([mean, rstd]), "gx", axis=0)

    depth, local_heads = w_qkv.shape[:2]
    head_size = w_qkv.shape[2] // 3
    width = local_heads * head_size
    w_q = w_qkv[:, :, :head_size].reshape(depth, width)
    w_k = w_qkv[:, :, head_size : 2 * head_size].reshape(depth, width)
    w_v = w_qkv[:, :, 2 * head_size :].reshape(depth, width)

    requests = cache_len.shape[0]
    share = gx_n // requests
    group = share * local_rows
    rows = share * piece
    part = rows // gy_n
    block = kv_cache.shape[1]
    old_keys, old_values = split_cache(kv_cache)

    queries, keys, values = [], [], []
    for c in range(CHUNKS):
        st = stats[:, :, c * piece : (c + 1) * piece]
        normed = (
            (gathered[c].astype(jnp.float32) - st[:, 0, :, None]) * st[:, 1, :, None] * ln_gain
        ).astype(jnp.bfloat16)
        normed = normed.reshape(gx_n * piece, depth)
        kv = [
            jnp.dot(normed, w, preferred_element_type=jnp.float32)
            .astype(jnp.bfloat16)
            .reshape(requests, rows, width)
            for w in (w_k, w_v)
        ]
        q = jnp.dot(normed, w_q, preferred_element_type=jnp.float32).astype(jnp.bfloat16)
        keys.append(scatter_gy(kv[0]))
        queries.append(sum_gy(q).reshape(requests, rows, local_heads, head_size))
        values.append(scatter_gy(kv[1]))

    flat = jnp.arange(rows, dtype=jnp.int32)
    tokens = [(flat // piece) * local_rows + c * piece + flat % piece for c in range(CHUNKS)]
    own = [lax.dynamic_slice_in_dim(t, gy * part, part) for t in tokens]
    own_tokens = jnp.concatenate(own)
    own_keys = jnp.concatenate(keys, axis=1)
    own_values = jnp.concatenate(values, axis=1)

    def whole(parts):
        full = lax.all_gather(parts, "gy", axis=0)
        full = full.reshape(gy_n, requests, CHUNKS, part, width).transpose(1, 2, 0, 3, 4)
        full = full.reshape(requests, CHUNKS, share, piece, width).transpose(0, 2, 1, 3, 4)
        return full.reshape(requests, group, width)

    fresh = jnp.stack([whole(own_keys), whole(own_values)], axis=2)
    window = min(group, block)
    padded = jnp.pad(fresh, ((0, 0), (window, window), (0, 0), (0, 0)))
    updated = kv_cache
    for r in range(requests):
        away = cache_len[r] - gy * block
        begin = jnp.clip(away, 0, block - window)
        taken = lax.dynamic_slice_in_dim(
            padded[r], jnp.clip(window + begin - away, 0, group + window), window
        )
        offset = begin - away + jnp.arange(window, dtype=jnp.int32)
        inside = (offset >= 0) & (offset < group)
        old = lax.dynamic_slice_in_dim(kv_cache[r], begin, window)
        new = jnp.where(inside[:, None, None], taken, old)
        updated = lax.dynamic_update_slice(updated, new[None], (r, begin, 0, 0))

    head_ids = lax.axis_index("gx") * local_heads + jnp.arange(local_heads, dtype=jnp.int32)
    slopes = jnp.exp2(-8.0 * (head_ids + 1).astype(jnp.float32) / (local_heads * gx_n))
    scale = 1.0 / math.sqrt(head_size)
    positions = gy * block + jnp.arange(block, dtype=jnp.int32)
    results = []
    full_keys = jnp.concatenate([old_keys, own_keys], axis=1)
    full_values = jnp.concatenate([old_values, own_values], axis=1)
    full_keys = full_keys.reshape(requests, -1, local_heads, head_size)
    full_values = full_values.reshape(requests, -1, local_heads, head_size)
    for c in range(CHUNKS):
        parts = []
        for r in range(requests):
            length = cache_len[r]
            places = jnp.concatenate([positions, length + own_tokens])
            distance = (length + tokens[c])[:, None] - places[None, :]
            cached = jnp.concatenate([positions < length, own_tokens >= 0])
            valid = (distance >= 0) & cached[None, :]
            parts.append(
                partial_attend(
                    queries[c][r], full_keys[r], full_values[r], valid, distance, slopes, scale
                )
            )
        top, total, accum = (jnp.stack(p) for p in zip(*parts))
        attn = combine(top, total, accum).reshape(requests * rows, width)
        projected = lax.psum_scatter(
            jnp.dot(attn, w_out, preferred_element_type=jnp.float32).astype(jnp.bfloat16),
            "gx",
            scatter_dimension=0,
            tiled=True,
        ).astype(jnp.float32)
        results.append(projected)
    mixed = (jnp.concatenate(results) + hidden_f).astype(jnp.bfloat16)
    return (mixed, updated)


def solution(mesh):
    in_specs = (
        P(("req", "gx"), "gy"),
        P("gy"),
        P("gy", "gx", None),
        P("gx", "gy"),
        P("req", "gy", None, "gx"),
        P("req"),
    )
    out_specs = (P(("req", "gx"), "gy"), P("req", "gy", None, "gx"))
    return jax.shard_map(shards, mesh=mesh, in_specs=in_specs, out_specs=out_specs, check_vma=False)
```

time: 565 us -> 374 us (0.66)
  waiting for transfers between devices: 251 us -> 132 us
  local copies, waits for them, and re-layouts: 163 us -> 84.3 us
  matrix products: 42.3 us -> 56.5 us
  other arithmetic: 67.9 us -> 58 us
  blocking collectives: 21.3 us -> 13.7 us
  starting transfers between devices: 0.38 us -> 7.7 us
    psum x2 -> x0, waiting for transfers between devices: 153 us -> none  [the longest x1 108 us: shards(): qkv = lax.psum(partial_value.astype(jnp.bfloat16), 'gy')]
    ppermute x0 -> x6, waiting for transfers between devices: none -> 107 us  [other(): return lax.ppermute(value, 'gy', [(0, 1), (1, 0)])]
    gather x2 -> x0, local copies, waits for them, and re-layouts: 69.9 us -> none  [write_cache(): taken = jnp.take(fresh_rows, jnp.clip(offset, 0, group - 1), axis=0)]
    all_gather x1 -> x3, waiting for transfers between devices: 53.3 us -> 0.02 us  [the longest x1 0.02 us: shards(): lax.all_gather(hidden[c * piece:(c + 1) * piece], 'gx', axis=0)]
    slice x6 -> x8, local copies, waits for them, and re-layouts: 60.8 us -> 34.1 us  [the longest x1 9.18 us: shards(): w_q = w_qkv[:, :, :head_size].reshape(depth, width)]
    reduce_scatter x1, waiting for transfers between devices: 44.7 us -> 24.6 us  [shards(): lax.psum_scatter(jnp.dot(attn, w_out, preferred_element_type=jnp.float32)...]
    reshape x1 -> x2, local copies, waits for them, and re-layouts: 2.99 us -> 20.7 us  [the longest x1 14.1 us: split_cache(): rows = cache.reshape(requests, 2 * block // size, size, width)]
    select_n x2 -> x4, other arithmetic: 21 us -> 5.28 us  [the longest x2 5.11 us: shards(): new = jnp.where(inside[:, None, None], taken, old)]
  transfers between devices with their start and end apart: 4 -> 10, of which waited for: 4 -> 5; matrix products, arithmetic and copies ran while one was open for 7% -> 48% of each run, Pallas kernels for 0% -> 0%
where the time goes in v1:
time: 374 us; the launch traced here: 367 us
  waiting for transfers between devices  132 us (35%)
  local copies, waits for them, and re-layouts  84.3 us (23%)
  other arithmetic  58 us (16%)
  matrix products  56.5 us (15%)
  between operations  15.6 us (4%)
  blocking collectives  13.7 us (4%)
  starting transfers between devices  7.7 us (2%)
    ppermute x6, waiting for transfers between devices, other(): return lax.ppermute(value, 'gy', [(0, 1), (1, 0)])  107 us
    reduce_scatter x1, waiting for transfers between devices, shards(): lax.psum_scatter(jnp.dot(attn, w_out, preferred_element_type=jnp.float32)...  24.6 us
    dot_general x2, matrix products, partial_attend(): jnp.einsum('chd,phd->chp', query, keys, preferred_element_type=jnp.float32)  17.5 us
    reduce_sum x2, other arithmetic, partial_attend(): totals = jnp.sum(weights, axis=-1)  16.7 us
    dot_general x2, matrix products, partial_attend(): jnp.einsum('chp,phd->chd', weights.astype(jnp.bfloat16), values, preferre...  14.4 us
    reshape x1, local copies, waits for them, and re-layouts, split_cache(): rows = cache.reshape(requests, 2 * block // size, size, width)  14.1 us
    all_gather x1, blocking collectives, shards(): stats = lax.all_gather(jnp.stack([mean, rstd]), 'gx', axis=0)  13.7 us
    unnamed x45, local copies, waits for them, and re-layouts  12.3 us
  transfers between devices with their start and end apart: 10, of which 5 were waited for; matrix products, arithmetic and copies ran while one was open for 48% of the time, Pallas kernels for 0%

profile of v1, /device:TPU:0, one launch (start us, length us, event | category | flops | bytes accessed | tf_op | source)
XLA Modules:
  0.0 367.3 jit_solution(9256548258325879200)
XLA Ops:
  7.2 8.6 %copy.166 = bf16[2,1088,2,1024]{3,2,1,0:T(2,128)(2,1)} copy(bf16[2,1088,2,1024]{3,2,1,0:T(2,128)(2,1)} %param.10) | data formatting | bytes 17825792
  15.9 0.4 convert_reduce_fusion
  16.3 3.0 collective-permute-start
  19.4 0.6 fusion.98
  20.0 1.2 broadcast_add_fusion.2
  21.3 1.2 broadcast_add_fusion
  22.5 1.2 fusion.69
  23.7 14.1 %reshape.413 = bf16[2,17,128,1024]{3,2,1,0:T(8,128)(2,1)} reshape(bf16[2,1088,2,1024]{3,2,1,0:T(2,128)(2,1)} %copy.166) | data formatting | bytes 17825792 | tf_op jit(solution)/shard_map/reshape | solution.py:63
  37.9 1.6 fusion.35
  39.5 1.5 subtract_convert_fusion.1
  41.1 1.5 subtract_convert_fusion
  42.6 6.1 %convert_bitcast_fusion = bf16[2,17,128,1024]{3,2,1,0:T(8,128)(2,1)S(1)} fusion(bf16[2,17,128,1024]{3,2,1,0:T(8,128)(2,1)} %reshape.413, s32[128]{0:T(128)S(1)} %fusion.89), kind=kOutput, calls=%fused_computation.16 | convolution fusion | flops 1145323520 | bytes 17826304 | tf_op jit(solution)/shard_map/ks,rbsd->rbkd/dot_general | solution.py:68
  48.6 4.6 %fusion.96 = (bf16[2,17,64,1024]{3,2,1,0:T(8,128)(2,1)}, bf16[2,17,64,1024]{3,2,1,0:T(8,128)(2,1)}) fusion(bf16[2,17,128,1024]{3,2,1,0:T(8,128)(2,1)S(1)} %convert_bitcast_fusion), kind=kLoop, calls=%fused_computation.159 | loop fusion | bytes 17825792 | tf_op jit(solution)/shard_map/slice | solution.py:71
  53.2 9.2 %fusion.93 = (bf16[2048,8,128]{2,1,0:T(8,128)(2,1)}, bf16[2048,8,128]{2,1,0:T(8,128)(2,1)}, bf16[2048,8,128]{2,1,0:T(8,128)(2,1)}) fusion(bf16[2048,8,384]{2,1,0:T(8,128)(2,1)} %param.8), kind=kLoop, calls=%fused_computation.156 | loop fusion | bytes 25165824 | tf_op jit(solution)/shard_map/slice | solution.py:107
  62.4 1.6 fusion.36
  64.0 6.6 %copy.90 = bf16[2,1088,1024]{1,2,0:T(8,128)(2,1)} copy(bf16[2,1088,1024]{2,1,0:T(8,128)(2,1)} %bitcast.129) | data formatting | bytes 8912896 | tf_op jit(solution)/shard_map/reshape | solution.py:71
  70.7 13.7 %all-gather.4 = f32[4,2,192]{2,1,0:T(2,128)S(1)} all-gather(f32[1,2,192]{2,1,0:T(2,128)S(1)} %maximum_bitcast_fusion), channel_id=3, replica_groups=mesh['req'=4,'gx'=4,'gy'=2] {'gx'}, dimensions={0}, use_global_device_ids=true | all-gather | bytes 7680 | tf_op jit(solution)/shard_map/all_gather | solution.py:102
  84.4 3.0 fusion.22
  87.5 0.1 copy-done.8
  87.5 3.4 fusion.37
  91.0 3.4 fusion.40
  94.7 2.0 collective-permute-start.1
  96.7 4.6 %fusion.43 = bf16[768,1024]{1,0:T(8,128)(2,1)} fusion(bf16[768,2048]{1,0:T(8,128)(2,1)S(1)} %bitcast.142, bf16[256,8,8,128]{3,2,1,0:T(8,128)(2,1)S(1)} %bitcast.136), kind=kOutput, calls=%fused_computation.62 | convolution fusion | flops 3222011904 | bytes 8912896 | tf_op jit(solution)/shard_map/dot_general | solution.py:132
  101.4 13.7 %collective-permute-done.2 = bf16[2,192,1024]{2,1,0:T(8,128)(2,1)S(1)} collective-permute-done((bf16[2,192,1024]{2,1,0:T(8,128)(2,1)S(1)}, bf16[2,192,1024]{2,1,0:T(8,128)(2,1)S(1)}, u32[]{:S(2)}, u32[]{:S(2)}) %collective-permute-start.2) | collective-permute-done | bytes 786464 | tf_op jit(solution)/shard_map/ppermute | solution.py:16
  115.1 1.3 add_convert_fusion.2
  116.5 0.3 all-gather.13.cloned.1.call-start
  116.8 2.2 copy.91
  119.0 20.6 %collective-permute-done.1 = bf16[2,192,1024]{2,1,0:T(8,128)(2,1)} collective-permute-done((bf16[2,192,1024]{2,1,0:T(8,128)(2,1)S(1)}, bf16[2,192,1024]{2,1,0:T(8,128)(2,1)}, u32[]{:S(2)}, u32[]{:S(2)}) %collective-permute-start.1) | collective-permute-done | bytes 786464 | tf_op jit(solution)/shard_map/ppermute | solution.py:16
  139.5 1.6 add_convert_fusion.3
  141.1 3.9 %fusion.34 = (bf16[1,1280,1024]{2,1,0:T(8,128)(2,1)}, bf16[1,1280,1024]{2,1,0:T(8,128)(2,1)S(1)}) fusion(bf16[2,1088,1024]{2,1,0:T(8,128)(2,1)} %bitcast.128, bf16[2,192,1024]{2,1,0:T(8,128)(2,1)S(1)} %add_convert_fusion.3), kind=kLoop, calls=%fused_computation.52 | loop fusion | flops 10485760 | bytes 10485760 | tf_op jit(solution)/shard_map/concatenate | solution.py:172
  145.0 4.4 %copy.89 = bf16[1,1280,1024]{1,2,0:T(8,128)(2,1)} copy(bf16[1,1280,1024]{2,1,0:T(8,128)(2,1)} %get-tuple-element.15) | data formatting | bytes 5242880 | tf_op jit(solution)/shard_map/slice | solution.py:185
  149.5 2.7 copy.95
  152.2 5.2 %fusion.33 = (bf16[1,1280,1024]{1,2,0:T(8,128)(2,1)S(1)}, bf16[1,1280,1024]{1,2,0:T(8,128)(2,1)}) fusion(bf16[2,1088,1024]{1,2,0:T(8,128)(2,1)} %copy.90, bf16[2,192,1024]{1,2,0:T(8,128)(2,1)} %copy.91), kind=kLoop, calls=%fused_computation.51 | loop fusion | flops 10485760 | bytes 10485760 | tf_op jit(solution)/shard_map/concatenate | solution.py:171
  157.4 21.8 %collective-permute-done.3 = bf16[768,1024]{1,0:T(8,128)(2,1)} collective-permute-done((bf16[768,1024]{1,0:T(8,128)(2,1)}, bf16[768,1024]{1,0:T(8,128)(2,1)}, u32[]{:S(2)}, u32[]{:S(2)}) %collective-permute-start.3) | collective-permute-done | bytes 1572896 | tf_op jit(solution)/shard_map/ppermute | solution.py:16
  179.3 2.5 add_convert_fusion.1
  181.8 1.0 slice_bitcast_fusion.1
  182.9 8.5 %fusion.100 = (f32[384,8]{0,1:T(8,128)S(1)}, f32[384,8,1280]{0,2,1:T(8,128)}) fusion(f32[384,1280]{0,1:T(8,128)S(1)} %copy-done.13, f32[8]{0:T(128)S(1)} %multiply_exponential_fusion, bf16[1280,8,128]{0,2,1:T(8,128)(2,1)S(1)} %bitcast.146, bf16[48,8,8,128]{3,2,1,0:T(8,128)(2,1)S(1)} %get-tuple-element.17, pred[384,1280]{0,1:T(8,128)(4,1)S(1)} %copy-done.16), kind=kOutput, calls=%fused_computation.163 | convolution fusion | flops 1026290688 | bytes 21606432 | tf_op jit(solution)/shard_map/chd,phd->chp/dot_general | solution.py:77
  191.4 8.3 %fusion.5 = f32[384,8]{0,1:T(8,128)S(1)} fusion(f32[384,8,1280]{0,2,1:T(8,128)} %get-tuple-element.37, f32[384,8]{0,1:T(8,128)S(1)} %get-tuple-element.36, pred[384,1280]{0,1:T(8,128)(4,1)S(1)} %copy-done.16), kind=kLoop, calls=%fused_computation.11 | loop fusion | flops 11793408 | bytes 16244736 | tf_op jit(solution)/shard_map/reduce_sum | solution.py:82
  199.8 7.3 %fusion.50 = f32[1,384,8,128]{1,3,2,0:T(8,128)S(1)} fusion(bf16[1280,8,128]{0,2,1:T(8,128)(2,1)S(1)} %bitcast.144, f32[384,8,1280]{0,2,1:T(8,128)} %get-tuple-element.37, f32[384,8]{0,1:T(8,128)S(1)} %get-tuple-element.36, pred[384,1280]{0,1:T(8,128)(4,1)} %fusion.35), kind=kOutput, calls=%fused_computation.73 | convolution fusion | flops 1018429440 | bytes 20426752 | tf_op jit(solution)/shard_map/chp,phd->chd/dot_general | solution.py:83
  207.1 9.0 %fusion.99 = (f32[384,8]{0,1:T(8,128)S(1)}, f32[384,8,1280]{0,2,1:T(8,128)}) fusion(f32[384,1280]{0,1:T(8,128)S(1)} %copy-done.12, f32[8]{0:T(128)S(1)} %multiply_exponential_fusion, bf16[1280,8,128]{0,2,1:T(8,128)(2,1)S(1)} %bitcast.145, bf16[48,8,8,128]{3,2,1,0:T(8,128)(2,1)S(1)} %copy-done.18, pred[384,1280]{0,1:T(8,128)(4,1)S(1)} %copy-done.14), kind=kOutput, calls=%fused_computation.162 | convolution fusion | flops 1026290688 | bytes 21606432 | tf_op jit(solution)/shard_map/chd,phd->chp/dot_general | solution.py:77
  216.1 8.3 %fusion.7 = f32[384,8]{0,1:T(8,128)S(1)} fusion(f32[384,8,1280]{0,2,1:T(8,128)} %get-tuple-element.35, f32[384,8]{0,1:T(8,128)S(1)} %get-tuple-element.34, pred[384,1280]{0,1:T(8,128)(4,1)} %fusion.36), kind=kLoop, calls=%fused_computation.13 | loop fusion | flops 11793408 | bytes 16244736 | tf_op jit(solution)/shard_map/reduce_sum | solution.py:82
  224.5 1.6 collective-permute-start.4
  226.1 7.1 %fusion.53 = f32[1,384,8,128]{1,3,2,0:T(8,128)S(1)} fusion(bf16[1280,8,128]{0,2,1:T(8,128)(2,1)S(1)} %bitcast.143, f32[384,8,1280]{0,2,1:T(8,128)} %get-tuple-element.35, f32[384,8]{0,1:T(8,128)S(1)} %get-tuple-element.34, pred[384,1280]{0,1:T(8,128)(4,1)S(1)} %copy-done.15), kind=kOutput, calls=%fused_computation.74 | convolution fusion | flops 1018429440 | bytes 20426752 | tf_op jit(solution)/shard_map/chp,phd->chd/dot_general | solution.py:83
  233.2 1.1 copy-done.4
  234.3 1.5 fusion.32
  235.8 0.5 collective-permute-start.5
  236.4 50.7 %collective-permute-done.5 = bf16[2,384,8,128]{1,3,2,0:T(8,128)(2,1)S(1)} collective-permute-done((bf16[2,384,8,128]{1,3,2,0:T(8,128)(2,1)}, bf16[2,384,8,128]{1,3,2,0:T(8,128)(2,1)S(1)}, u32[]{:S(2)}, u32[]{:S(2)}) %collective-permute-start.5) | collective-permute-done | bytes 1572896 | tf_op jit(solution)/shard_map/ppermute | solution.py:16
  287.2 1.1 copy-done.17
  288.3 2.6 add_convert_fusion
  290.9 1.4 copy.99
  292.2 7.0 %convolution_convert_fusion = bf16[768,2048]{1,0:T(8,128)(2,1)} fusion(bf16[1024,2048]{1,0:T(8,128)(2,1)} %param.9, bf16[96,8,8,128]{3,2,1,0:T(8,128)(2,1)S(1)} %bitcast.149), kind=kOutput, calls=%fused_computation.42 | convolution fusion | flops 3222798336 | bytes 8912896 | tf_op jit(solution)/shard_map/dot_general | solution.py:191
  300.5 7.7 %fusion.95 = (bf16[1,1088,2,1024]{3,2,1,0:T(2,128)(2,1)S(1)}, bf16[1,1088,2,1024]{3,2,1,0:T(2,128)(2,1)S(1)}) fusion(bf16[2,1088,2,1024]{3,2,1,0:T(2,128)(2,1)} %copy.166), kind=kLoop, calls=%fused_computation.158 | loop fusion | bytes 17825792 | tf_op jit(solution)/shard_map/slice | solution.py:162
  308.2 3.8 %constant_dynamic-slice_fusion = (bf16[1,384,2,1024]{3,2,1,0:T(2,128)(2,1)}, bf16[1,384,2,1024]{3,2,1,0:T(2,128)(2,1)}) fusion(bf16[1,1088,2,1024]{3,2,1,0:T(2,128)(2,1)S(1)} %get-tuple-element.9, s32[]{:T(128)S(6)} %min.15, bf16[1,1088,2,1024]{3,2,1,0:T(2,128)(2,1)S(1)} %get-tuple-element.10, s32[]{:T(128)S(6)} %min.13), kind=kLoop, calls=%fused_computation.136 | loop fusion | bytes 6291464 | tf_op jit(solution)/shard_map/dynamic_slice | solution.py:162
  312.0 2.7 copy.100
  314.7 1.7 copy.101
  316.4 0.3 copy-done.3
  316.7 1.5 fusion.9
  318.1 4.9 %fusion.94 = (bf16[1,1152,2,1024]{3,1,0,2:T(8,128)(2,1)}, bf16[1,1152,2,1024]{3,1,0,2:T(8,128)(2,1)}) fusion(bf16[2,1152,2,1024]{3,1,0,2:T(8,128)(2,1)S(1)} %fusion.9), kind=kLoop, calls=%fused_computation.157 | loop fusion | bytes 18874368 | tf_op jit(solution)/shard_map/slice | solution.py:158
  323.0 2.8 copy_select_fusion.1
  325.8 2.3 copy_select_fusion
  328.1 2.8 copy_dynamic-update-slice_fusion.1
  330.9 2.8 copy_dynamic-update-slice_fusion
  333.7 24.6 %reduce-scatter.2.cloned.1.call-done = bf16[192,2048]{1,0:T(8,128)(2,1)} async-done(((bf16[768,2048]{1,0:T(8,128)(2,1)}), bf16[192,2048]{1,0:T(8,128)(2,1)}) %reduce-scatter.2.cloned.1.call-update) | async-done | bytes 786448 | tf_op jit(solution)/shard_map/reduce_scatter | solution.py:190
  358.2 2.3 fusion.47
  (72 shorter events, 1.0 us)
Async XLA Ops:
  7.2 8.7 %copy-start = (bf16[192,2048]{1,0:T(8,128)(2,1)S(1)}, bf16[192,2048]{1,0:T(8,128)(2,1)}, u32[]{:S(2)}) copy-start(bf16[192,2048]{1,0:T(8,128)(2,1)} %param.6) | copy-start | bytes 2359300
  7.2 12.2 %copy-start.20 = (s32[2]{0:T(128)S(1)}, s32[2]{0:T(128)}, u32[]{:S(2)}) copy-start(s32[2]{0:T(128)} %param.11) | copy-start | bytes 28
  7.2 77.2 %all-gather.9.cloned.1.call-start = ((), (), s32[]{:S(2)}) async-start(), calls=%async_computation.2 | async-start | bytes 3932160 | tf_op jit(solution)/shard_map/all_gather | solution.py:97
  15.8 296.2 %all-gather.11.cloned.1.call-start = ((), (), s32[]{:S(2)}) async-start(), calls=%async_computation.3 | async-start | bytes 2359296 | tf_op jit(solution)/shard_map/all_gather | solution.py:145
  16.3 54.3 %collective-permute-start = (f32[2,192]{1,0:T(2,128)S(1)}, f32[2,192]{1,0:T(2,128)S(1)}, u32[]{:S(2)}, u32[]{:S(2)}) collective-permute-start(f32[2,192]{1,0:T(2,128)S(1)} %pad_maximum_fusion.5), channel_id=1, source_target_pairs={{0,1},{1,0},{2,3},{3,2},{4,5},{5,4},{6,7},{7,6},{8,9},{9,8},{10,11... | collective-permute-start | bytes 4616 | tf_op jit(solution)/shard_map/ppermute | solution.py:16
  64.0 20.4 %copy-start.19 = (f32[2048]{0:T(1024)S(1)}, f32[2048]{0:T(1024)}, u32[]{:S(2)}) copy-start(f32[2048]{0:T(1024)} %param.7) | copy-start | bytes 24580
  84.4 3.1 copy-start.8
  87.5 3.4 copy-start.7
  94.4 2.3 copy-start.6
  94.6 20.5 %collective-permute-start.2 = (bf16[2,192,1024]{2,1,0:T(8,128)(2,1)S(1)}, bf16[2,192,1024]{2,1,0:T(8,128)(2,1)S(1)}, u32[]{:S(2)}, u32[]{:S(2)}) collective-permute-start(bf16[2,192,1024]{2,1,0:T(8,128)(2,1)S(1)} %broadcast_select_fusion), channel_id=1, source_target_pairs={{0,1},{1,0},{2,3},{3,2},{4,5},{5,4},{6,7},{7,6},{8,9},{9,8},{10,11... | collective-permute-start | bytes 2359304 | tf_op jit(solution)/shard_map/ppermute | solution.py:16
  94.7 44.9 %collective-permute-start.1 = (bf16[2,192,1024]{2,1,0:T(8,128)(2,1)S(1)}, bf16[2,192,1024]{2,1,0:T(8,128)(2,1)}, u32[]{:S(2)}, u32[]{:S(2)}) collective-permute-start(bf16[2,192,1024]{2,1,0:T(8,128)(2,1)S(1)} %broadcast_select_fusion.1), channel_id=1, source_target_pairs={{0,1},{1,0},{2,3},{3,2},{4,5},{5,4},{6,7},{7,6},{8,9},{9,8},{10,11... | collective-permute-start | bytes 2359304 | tf_op jit(solution)/shard_map/ppermute | solution.py:16
  101.3 77.9 %collective-permute-start.3 = (bf16[768,1024]{1,0:T(8,128)(2,1)}, bf16[768,1024]{1,0:T(8,128)(2,1)}, u32[]{:S(2)}, u32[]{:S(2)}) collective-permute-start(bf16[768,1024]{1,0:T(8,128)(2,1)} %fusion.43), channel_id=1, source_target_pairs={{0,1},{1,0},{2,3},{3,2},{4,5},{5,4},{6,7},{7,6},{8,9},{9,8},{10,11... | collective-permute-start | bytes 4718600 | tf_op jit(solution)/shard_map/ppermute | solution.py:16
  116.5 198.3 %all-gather.13.cloned.1.call-start = ((), (), s32[]{:S(2)}) async-start(), calls=%async_computation.4 | async-start | bytes 2359296 | tf_op jit(solution)/shard_map/all_gather | solution.py:145
  141.1 3.9 %copy-start.2 = (bf16[2,192,1024]{2,1,0:T(8,128)(2,1)}, bf16[2,192,1024]{2,1,0:T(8,128)(2,1)S(1)}, u32[]{:S(2)}) copy-start(bf16[2,192,1024]{2,1,0:T(8,128)(2,1)S(1)} %add_convert_fusion.3) | copy-start | bytes 2359300
  157.4 25.4 %copy-start.13 = (f32[384,1280]{0,1:T(8,128)S(1)}, f32[384,1280]{0,1:T(8,128)}, u32[]{:S(2)}) copy-start(f32[384,1280]{0,1:T(8,128)} %subtract_convert_fusion.1) | copy-start | bytes 5898244
  157.4 25.4 %copy-start.16 = (pred[384,1280]{0,1:T(8,128)(4,1)S(1)}, pred[384,1280]{0,1:T(8,128)(4,1)}, u32[]{:S(2)}) copy-start(pred[384,1280]{0,1:T(8,128)(4,1)} %fusion.35) | copy-start | bytes 1474564
  191.4 8.4 %copy-start.10 = (bf16[1,1280,1024]{1,2,0:T(8,128)(2,1)S(1)}, bf16[1,1280,1024]{1,2,0:T(8,128)(2,1)}, u32[]{:S(2)}) copy-start(bf16[1,1280,1024]{1,2,0:T(8,128)(2,1)} %copy.89) | copy-start | bytes 7864324
  199.7 7.4 %copy-start.11 = (bf16[1,1280,1024]{1,2,0:T(8,128)(2,1)S(1)}, bf16[1,1280,1024]{1,2,0:T(8,128)(2,1)}, u32[]{:S(2)}) copy-start(bf16[1,1280,1024]{1,2,0:T(8,128)(2,1)} %get-tuple-element.14) | copy-start | bytes 7864324
  199.7 7.4 %copy-start.12 = (f32[384,1280]{0,1:T(8,128)S(1)}, f32[384,1280]{0,1:T(8,128)}, u32[]{:S(2)}) copy-start(f32[384,1280]{0,1:T(8,128)} %subtract_convert_fusion) | copy-start | bytes 5898244
  199.7 7.4 %copy-start.14 = (pred[384,1280]{0,1:T(8,128)(4,1)S(1)}, pred[384,1280]{0,1:T(8,128)(4,1)}, u32[]{:S(2)}) copy-start(pred[384,1280]{0,1:T(8,128)(4,1)} %fusion.36) | copy-start | bytes 1474564
  199.8 7.4 %copy-start.18 = (bf16[48,8,8,128]{3,2,1,0:T(8,128)(2,1)S(1)}, bf16[48,8,8,128]{3,2,1,0:T(8,128)(2,1)}, u32[]{:S(2)}) copy-start(bf16[48,8,8,128]{3,2,1,0:T(8,128)(2,1)} %get-tuple-element.18) | copy-start | bytes 2359300
  216.1 10.0 %copy-start.9 = (bf16[1,1280,1024]{1,2,0:T(8,128)(2,1)S(1)}, bf16[1,1280,1024]{1,2,0:T(8,128)(2,1)}, u32[]{:S(2)}) copy-start(bf16[1,1280,1024]{1,2,0:T(8,128)(2,1)} %copy.95) | copy-start | bytes 7864324
  216.1 10.0 %copy-start.15 = (pred[384,1280]{0,1:T(8,128)(4,1)S(1)}, pred[384,1280]{0,1:T(8,128)(4,1)}, u32[]{:S(2)}) copy-start(pred[384,1280]{0,1:T(8,128)(4,1)} %fusion.36) | copy-start | bytes 1474564
  224.5 8.7 %collective-permute-start.4 = (f32[2,2,384,8]{2,3,1,0:T(8,128)S(1)}, f32[2,2,384,8]{2,3,1,0:T(8,128)S(1)}, u32[]{:S(2)}, u32[]{:S(2)}) collective-permute-start(f32[2,2,384,8]{2,3,1,0:T(8,128)S(1)} %pad_maximum_fusion.2), channel_id=1, source_target_pairs={{0,1},{1,0},{2,3},{3,2},{4,5},{5,4},{6,7},{7,6},{8,9},{9,8},{10,11... | collective-permute-start | bytes 147464 | tf_op jit(solution)/shard_map/ppermute | solution.py:16
  233.2 1.1 copy-start.4
  235.8 51.3 %collective-permute-start.5 = (bf16[2,384,8,128]{1,3,2,0:T(8,128)(2,1)}, bf16[2,384,8,128]{1,3,2,0:T(8,128)(2,1)S(1)}, u32[]{:S(2)}, u32[]{:S(2)}) collective-permute-start(bf16[2,384,8,128]{1,3,2,0:T(8,128)(2,1)} %fusion.32), channel_id=1, source_target_pairs={{0,1},{1,0},{2,3},{3,2},{4,5},{5,4},{6,7},{7,6},{8,9},{9,8},{10,11... | collective-permute-start | bytes 4718600 | tf_op jit(solution)/shard_map/ppermute | solution.py:16
  236.4 121.9 %reduce-scatter.2.cloned.1.call-start = ((), (), s32[]{:S(2)}) async-start(), calls=%async_computation.1 | async-start | bytes 3932160 | tf_op jit(solution)/shard_map/reduce_scatter | solution.py:190
  287.2 1.1 copy-start.17
  314.7 1.9 copy-start.3
  323.0 2.9 copy-start.5
  328.1 30.1 %copy-start.1 = (bf16[192,2048]{1,0:T(8,128)(2,1)S(1)}, bf16[192,2048]{1,0:T(8,128)(2,1)}, u32[]{:S(2)}) copy-start(bf16[192,2048]{1,0:T(8,128)(2,1)} %param.6) | copy-start | bytes 2359300
Sparse Core Ops, SparseCore 0:
  16.0 66.2 all-gather.8
  116.6 41.8 all-gather.10
  236.5 43.0 all-gather.12
  299.4 58.7 reduce-scatter.1

commit v2 on v1

--- a/solution.py
+++ b/solution.py
@@ -1,12 +1,15 @@
+import functools
 import math
 
 import jax
 import jax.numpy as jnp
 from jax import lax
+from jax.experimental import pallas as pl
+from jax.experimental.pallas import tpu as pltpu
 from jax.sharding import PartitionSpec as P
 
 D = 4096
-CHUNKS = 1
+CHUNKS = 2
 
 norm_eps = 1e-05
 floor_score = -1e30
@@ -36,24 +39,22 @@
     return lax.psum_scatter(value, "gy", scatter_dimension=1, tiled=True)
 
 
-def combine(top, total, accum):
+def combine(part, level):
+    requests, rows, heads = level.shape
+    part = part.reshape(requests, rows, heads, -1)
     if lax.axis_size("gy") == 2:
-        safe = jnp.where(total > 0, total, 1.0)
-        part = (accum / safe[..., None]).astype(jnp.bfloat16)
-        stats = jnp.stack([top, total])
-        far_stats = other(stats)
-        far_part = other(part)
-        overall = jnp.maximum(top, far_stats[0])
-        mine = jnp.exp(top - overall) * total
-        far = jnp.exp(far_stats[0] - overall) * far_stats[1]
+        far_level = other(level)
+        far_part = other(part.reshape(requests, rows, -1)).reshape(part.shape)
+        overall = jnp.maximum(level, far_level)
+        mine, far = jnp.exp(level - overall), jnp.exp(far_level - overall)
         joined = mine + far
         return (
             part.astype(jnp.float32) * (mine / joined)[..., None]
             + far_part.astype(jnp.float32) * (far / joined)[..., None]
         ).astype(jnp.bfloat16)
-    factor = jnp.exp(top - lax.pmax(top, "gy"))
-    totals = lax.psum(total * factor, "gy")
-    accums = lax.psum((accum * factor[..., None]).astype(jnp.bfloat16), "gy")
+    factor = jnp.exp(level - lax.pmax(level, "gy"))
+    totals = lax.psum(factor, "gy")
+    accums = lax.psum((part.astype(jnp.float32) * factor[..., None]).astype(jnp.bfloat16), "gy")
     return (accums.astype(jnp.float32) / totals[..., None]).astype(jnp.bfloat16)
 
 
@@ -73,17 +74,76 @@
     )
 
 
-def partial_attend(query, keys, values, valid, distance, slopes, scale):
-    scores = jnp.einsum("chd,phd->chp", query, keys, preferred_element_type=jnp.float32) * scale
-    scores = scores - slopes[None, :, None] * distance.astype(jnp.float32)[:, None, :]
-    scores = jnp.where(valid[:, None, :], scores, floor_score)
-    highest = jnp.max(scores, axis=-1)
-    weights = jnp.where(valid[:, None, :], jnp.exp(scores - highest[..., None]), 0.0)
-    totals = jnp.sum(weights, axis=-1)
-    accum = jnp.einsum(
-        "chp,phd->chd", weights.astype(jnp.bfloat16), values, preferred_element_type=jnp.float32
-    )
-    return (highest, totals, accum)
+def attend_kernel(
+    scale, info, slopes, q_ref, ok_ref, ov_ref, nk_ref, nv_ref, c_ref, t_ref, part_ref, level_ref
+):
+    r, h = pl.program_id(0), pl.program_id(1)
+    slope = slopes[h]
+    away = info[0] - info[1 + r]
+    block = ok_ref.shape[1]
+    offset = lax.broadcasted_iota(jnp.int32, (1, block), 1) + away
+    bias = jnp.where(offset < 0, slope * offset.astype(jnp.float32), floor_score)
+    dims = (((1,), (1,)), ((), ()))
+    q = q_ref[0]
+    old = lax.dot_general(q, ok_ref[0], dims, preferred_element_type=jnp.float32) * scale + bias
+    token = t_ref[...]
+    new = lax.dot_general(q, nk_ref[0], dims, preferred_element_type=jnp.float32) * scale
+    new = jnp.where(token <= c_ref[...], new + slope * token.astype(jnp.float32), floor_score)
+    top = jnp.maximum(jnp.max(old, axis=1, keepdims=True), jnp.max(new, axis=1, keepdims=True))
+    top = jnp.maximum(top, 0.1 * floor_score)
+    old = jnp.exp(old - top)
+    new = jnp.exp(new - top)
+    total = jnp.sum(old, axis=1, keepdims=True) + jnp.sum(new, axis=1, keepdims=True)
+    accum = jnp.dot(old.astype(jnp.bfloat16), ov_ref[0], preferred_element_type=jnp.float32)
+    accum += jnp.dot(new.astype(jnp.bfloat16), nv_ref[0], preferred_element_type=jnp.float32)
+    some = total > 0
+    safe = jnp.where(some, total, 1.0)
+    part_ref[0] = (accum / safe).astype(part_ref.dtype)
+    level = jnp.where(some, top + jnp.log(safe), floor_score)
+    lane = lax.broadcasted_iota(jnp.int32, level_ref.shape[1:], 1)
+
+    @pl.when(h == 0)
+    def _():
+        level_ref[...] = jnp.zeros_like(level_ref)
+
+    level_ref[0] = jnp.where(lane == h, level, level_ref[0])
+
+
+def attend(info, slopes, q, old_k, old_v, new_k, new_v, tokens, own_tokens, heads):
+    requests, rows, width = q.shape
+    size = width // heads
+    head = lambda n: pl.BlockSpec((1, n, size), lambda r, h, *_: (r, 0, h))
+    fixed = lambda shape: pl.BlockSpec(shape, lambda r, h, *_: (0, 0))
+    block, own = old_k.shape[1], new_k.shape[1]
+    lanes = 128
+    part, level = pl.pallas_call(
+        functools.partial(attend_kernel, 1.0 / math.sqrt(size)),
+        grid_spec=pltpu.PrefetchScalarGridSpec(
+            num_scalar_prefetch=2,
+            grid=(requests, heads),
+            in_specs=[
+                head(rows),
+                head(block),
+                head(block),
+                head(own),
+                head(own),
+                fixed((rows, 1)),
+                fixed((1, own)),
+            ],
+            out_specs=[head(rows), pl.BlockSpec((1, rows, lanes), lambda r, h, *_: (r, 0, 0))],
+        ),
+        out_shape=[
+            jax.ShapeDtypeStruct((requests, rows, width), jnp.bfloat16),
+            jax.ShapeDtypeStruct((requests, rows, lanes), jnp.float32),
+        ],
+        compiler_params=pltpu.CompilerParams(vmem_limit_bytes=32 * 1024 * 1024),
+        cost_estimate=pl.CostEstimate(
+            flops=4 * requests * rows * (block + own) * width,
+            bytes_accessed=4 * requests * (block + own + rows) * width,
+            transcendentals=requests * rows * (block + own) * heads,
+        ),
+    )(info, slopes, q, old_k, old_v, new_k, new_v, tokens[:, None], own_tokens[None, :])
+    return part, level[:, :, :heads]
 
 
 def shards(hidden, ln_gain, w_qkv, w_out, kv_cache, cache_len):
@@ -112,10 +172,8 @@
     share = gx_n // requests
     group = share * local_rows
     rows = share * piece
-    part = rows // gy_n
+    own_rows = rows // gy_n
     block = kv_cache.shape[1]
-    old_keys, old_values = split_cache(kv_cache)
-
     queries, keys, values = [], [], []
     for c in range(CHUNKS):
         st = stats[:, :, c * piece : (c + 1) * piece]
@@ -130,24 +188,30 @@
             for w in (w_k, w_v)
         ]
         q = jnp.dot(normed, w_q, preferred_element_type=jnp.float32).astype(jnp.bfloat16)
+        if c == 0:
+            q, kv_cache = lax.optimization_barrier((q, kv_cache))
         keys.append(scatter_gy(kv[0]))
-        queries.append(sum_gy(q).reshape(requests, rows, local_heads, head_size))
         values.append(scatter_gy(kv[1]))
+        queries.append(sum_gy(q).reshape(requests, rows, width))
+    old_keys, old_values = split_cache(kv_cache)
 
     flat = jnp.arange(rows, dtype=jnp.int32)
     tokens = [(flat // piece) * local_rows + c * piece + flat % piece for c in range(CHUNKS)]
-    own = [lax.dynamic_slice_in_dim(t, gy * part, part) for t in tokens]
+    own = [lax.dynamic_slice_in_dim(t, gy * own_rows, own_rows) for t in tokens]
     own_tokens = jnp.concatenate(own)
     own_keys = jnp.concatenate(keys, axis=1)
     own_values = jnp.concatenate(values, axis=1)
 
     def whole(parts):
         full = lax.all_gather(parts, "gy", axis=0)
-        full = full.reshape(gy_n, requests, CHUNKS, part, width).transpose(1, 2, 0, 3, 4)
+        full = full.reshape(gy_n, requests, CHUNKS, own_rows, width).transpose(1, 2, 0, 3, 4)
         full = full.reshape(requests, CHUNKS, share, piece, width).transpose(0, 2, 1, 3, 4)
         return full.reshape(requests, group, width)
 
-    fresh = jnp.stack([whole(own_keys), whole(own_values)], axis=2)
+    sent_keys, sent_values, queries[-1] = lax.optimization_barrier(
+        (own_keys, own_values, queries[-1])
+    )
+    fresh = jnp.stack([whole(sent_keys), whole(sent_values)], axis=2)
     window = min(group, block)
     padded = jnp.pad(fresh, ((0, 0), (window, window), (0, 0), (0, 0)))
     updated = kv_cache
@@ -165,28 +229,22 @@
 
     head_ids = lax.axis_index("gx") * local_heads + jnp.arange(local_heads, dtype=jnp.int32)
     slopes = jnp.exp2(-8.0 * (head_ids + 1).astype(jnp.float32) / (local_heads * gx_n))
-    scale = 1.0 / math.sqrt(head_size)
-    positions = gy * block + jnp.arange(block, dtype=jnp.int32)
+    info = jnp.concatenate([(gy * block)[None].astype(jnp.int32), cache_len])
     results = []
-    full_keys = jnp.concatenate([old_keys, own_keys], axis=1)
-    full_values = jnp.concatenate([old_values, own_values], axis=1)
-    full_keys = full_keys.reshape(requests, -1, local_heads, head_size)
-    full_values = full_values.reshape(requests, -1, local_heads, head_size)
     for c in range(CHUNKS):
-        parts = []
-        for r in range(requests):
-            length = cache_len[r]
-            places = jnp.concatenate([positions, length + own_tokens])
-            distance = (length + tokens[c])[:, None] - places[None, :]
-            cached = jnp.concatenate([positions < length, own_tokens >= 0])
-            valid = (distance >= 0) & cached[None, :]
-            parts.append(
-                partial_attend(
-                    queries[c][r], full_keys[r], full_values[r], valid, distance, slopes, scale
-                )
-            )
-        top, total, accum = (jnp.stack(p) for p in zip(*parts))
-        attn = combine(top, total, accum).reshape(requests * rows, width)
+        part, level = attend(
+            info,
+            slopes,
+            queries[c],
+            old_keys,
+            old_values,
+            own_keys,
+            own_values,
+            tokens[c],
+            own_tokens,
+            local_heads,
+        )
+        attn = combine(part, level).reshape(requests * rows, width)
         projected = lax.psum_scatter(
             jnp.dot(attn, w_out, preferred_element_type=jnp.float32).astype(jnp.bfloat16),
             "gx",

time: 374 us -> 357 us (0.955); the launches traced: 367 us -> 356 us
  other arithmetic: 58 us -> 19.7 us
  Pallas kernels: 0 us -> 33.8 us
  matrix products: 56.5 us -> 30.2 us
  waiting for transfers between devices: 132 us -> 142 us
  starting transfers between devices: 7.7 us -> 15.1 us
    all_gather x1 -> x2, waiting for transfers between devices: 0.02 us -> 51.3 us  [shards(): lax.all_gather(hidden[c * piece:(c + 1) * piece], 'gx', axis=0)]
    pallas_call x0 -> x2, Pallas kernels: none -> 33.8 us  [attend(): pl.pallas_call(functools.partial(attend_kernel, 1.0 / math.sqrt(size)), g...]
    dot_general x4 -> x0, matrix products: 31.9 us -> none  [the longest x2 17.5 us: partial_attend(): jnp.einsum('chd,phd->chp', query, keys, preferred_element_type=jnp.float32)]
    ppermute x6 -> x11, waiting for transfers between devices: 107 us -> 76.6 us  [other(): return lax.ppermute(value, 'gy', [(0, 1), (1, 0)])]
    optimization_barrier x0 -> x2, local copies, waits for them, and re-layouts: none -> 18.5 us  [shards(): q, kv_cache = lax.optimization_barrier((q, kv_cache))]
    reduce_sum x2 -> x0, other arithmetic: 16.7 us -> none  [partial_attend(): totals = jnp.sum(weights, axis=-1)]
    reduce_scatter x1 -> x2, waiting for transfers between devices: 24.6 us -> 13.2 us  [shards(): lax.psum_scatter(jnp.dot(attn, w_out, preferred_element_type=jnp.float32)...]
    concatenate x4, other arithmetic: 9.31 us -> 2.11 us  [the longest x1 1.03 us: shards(): own_values = jnp.concatenate(values, axis=1)]
  transfers between devices with their start and end apart: 10 -> 17, of which waited for: 5 -> 10; matrix products, arithmetic and copies ran while one was open for 48% -> 29% of each run, Pallas kernels for 0% -> 9%
where the time goes in v2:
time: 357 us; the launch traced here: 356 us
  waiting for transfers between devices  142 us (40%)
  local copies, waits for them, and re-layouts  87.2 us (24%)
  Pallas kernels  33.8 us (9%)
  matrix products  30.2 us (8%)
  other arithmetic  19.7 us (6%)
  between operations  15.7 us (4%)
  starting transfers between devices  15.1 us (4%)
  blocking collectives  12.4 us (3%)
    ppermute x11, waiting for transfers between devices, other(): return lax.ppermute(value, 'gy', [(0, 1), (1, 0)])  76.6 us
    all_gather x2, waiting for transfers between devices, shards(): lax.all_gather(hidden[c * piece:(c + 1) * piece], 'gx', axis=0)  51.3 us
    pallas_call x2, Pallas kernels, attend(): pl.pallas_call(functools.partial(attend_kernel, 1.0 / math.sqrt(size)), g...  33.8 us
    optimization_barrier x2, local copies, waits for them, and re-layouts, shards(): q, kv_cache = lax.optimization_barrier((q, kv_cache))  18.5 us
    ppermute x11, starting transfers between devices, other(): return lax.ppermute(value, 'gy', [(0, 1), (1, 0)])  14.4 us
    reshape x1, local copies, waits for them, and re-layouts, split_cache(): rows = cache.reshape(requests, 2 * block // size, size, width)  14.1 us
    reduce_scatter x2, waiting for transfers between devices, shards(): lax.psum_scatter(jnp.dot(attn, w_out, preferred_element_type=jnp.float32)...  13.2 us
    all_gather x1, blocking collectives, shards(): stats = lax.all_gather(jnp.stack([mean, rstd]), 'gx', axis=0)  12.4 us
  transfers between devices with their start and end apart: 17, of which 10 were waited for; matrix products, arithmetic and copies ran while one was open for 29% of the time, Pallas kernels for 9%

profile of v2, /device:TPU:0, one launch (start us, length us, event | category | flops | bytes accessed | tf_op | source)
XLA Modules:
  0.0 356.0 jit_solution(4707056933242436630)
XLA Ops:
  7.2 8.6 %copy.89 = bf16[2,1088,2,1024]{3,2,1,0:T(2,128)(2,1)} copy(bf16[2,1088,2,1024]{3,2,1,0:T(2,128)(2,1)} %param.10) | data formatting | bytes 17825792 | tf_op jit(solution)/shard_map/optimization_barrier | solution.py:192
  15.8 0.9 fusion.89
  16.8 0.7 all-gather.13.cloned.1.call-update
  18.0 3.0 collective-permute-start
  21.3 9.2 %fusion.85 = (bf16[2048,8,128]{2,1,0:T(8,128)(2,1)}, bf16[2048,8,128]{2,1,0:T(8,128)(2,1)}, bf16[2048,8,128]{2,1,0:T(8,128)(2,1)}) fusion(bf16[2048,8,384]{2,1,0:T(8,128)(2,1)} %param.8), kind=kLoop, calls=%fused_computation.134 | loop fusion | bytes 25165824 | tf_op jit(solution)/shard_map/slice | solution.py:167
  30.7 12.4 %all-gather.5 = f32[4,2,192]{2,1,0:T(2,128)S(1)} all-gather(f32[1,2,192]{2,1,0:T(2,128)S(1)} %maximum_bitcast_fusion), channel_id=3, replica_groups=mesh['req'=4,'gx'=4,'gy'=2] {'gx'}, dimensions={0}, use_global_device_ids=true | all-gather | bytes 7680 | tf_op jit(solution)/shard_map/all_gather | solution.py:162
  43.1 13.8 %all-gather.11.cloned.1.call-done = bf16[384,2048]{1,0:T(8,128)(2,1)} async-done(((bf16[96,2048]{1,0:T(8,128)(2,1)}), bf16[384,2048]{1,0:T(8,128)(2,1)}) %all-gather.11.cloned.1.call-update) | async-done | bytes 1572880 | tf_op jit(solution)/shard_map/all_gather | solution.py:157
  56.9 37.6 %all-gather.13.cloned.1.call-done = bf16[384,2048]{1,0:T(8,128)(2,1)} async-done(((bf16[96,2048]{1,0:T(8,128)(2,1)}), bf16[384,2048]{1,0:T(8,128)(2,1)}) %all-gather.13.cloned.1.call-update) | async-done | bytes 1572880 | tf_op jit(solution)/shard_map/all_gather | solution.py:157
  94.4 3.0 fusion.27
  97.5 1.8 fusion.43
  99.3 1.8 fusion.40
  101.5 1.8 fusion.49
  103.3 1.8 fusion.46
  105.2 1.5 collective-permute-start.3
  106.8 0.6 collective-permute-start.2
  107.4 0.8 broadcast_select_fusion
  108.2 1.5 collective-permute-start.5
  109.7 0.8 broadcast_select_fusion.1
  110.5 0.6 collective-permute-start.4
  111.0 1.8 fusion.37
  112.8 1.5 collective-permute-start.8
  114.4 2.9 collective-permute-done.3
  117.5 8.2 %collective-permute-done.2 = bf16[2,96,1024]{2,1,0:T(8,128)(2,1)S(1)} collective-permute-done((bf16[2,96,1024]{2,1,0:T(8,128)(2,1)S(1)}, bf16[2,96,1024]{2,1,0:T(8,128)(2,1)S(1)}, u32[]{:S(2)}, u32[]{:S(2)}) %collective-permute-start.2) | collective-permute-done | bytes 393248 | tf_op jit(solution)/shard_map/ppermute | solution.py:19
  125.9 0.9 pad_maximum_fusion.nk_ref
  126.8 7.3 %collective-permute-done.5 = bf16[2,96,1024]{2,1,0:T(8,128)(2,1)S(1)} collective-permute-done((bf16[2,96,1024]{2,1,0:T(8,128)(2,1)}, bf16[2,96,1024]{2,1,0:T(8,128)(2,1)S(1)}, u32[]{:S(2)}, u32[]{:S(2)}) %collective-permute-start.5) | collective-permute-done | bytes 393248 | tf_op jit(solution)/shard_map/ppermute | solution.py:19
  134.3 8.2 %collective-permute-done.4 = bf16[2,96,1024]{2,1,0:T(8,128)(2,1)S(1)} collective-permute-done((bf16[2,96,1024]{2,1,0:T(8,128)(2,1)}, bf16[2,96,1024]{2,1,0:T(8,128)(2,1)S(1)}, u32[]{:S(2)}, u32[]{:S(2)}) %collective-permute-start.4) | collective-permute-done | bytes 393248 | tf_op jit(solution)/shard_map/ppermute | solution.py:19
  142.7 1.0 pad_maximum_fusion.1.nv_ref
  143.8 14.4 %collective-permute-done.8 = bf16[384,1024]{1,0:T(8,128)(2,1)} collective-permute-done((bf16[384,1024]{1,0:T(8,128)(2,1)S(1)}, bf16[384,1024]{1,0:T(8,128)(2,1)}, u32[]{:S(2)}, u32[]{:S(2)}) %collective-permute-start.8) | collective-permute-done | bytes 786464 | tf_op jit(solution)/shard_map/ppermute | solution.py:19
  158.2 1.4 add_convert_fusion
  159.9 4.5 %fusion.34 = bf16[384,1024]{1,0:T(8,128)(2,1)S(1)} fusion(bf16[384,2048]{1,0:T(8,128)(2,1)} %bitcast.160, bf16[256,8,8,128]{3,2,1,0:T(8,128)(2,1)} %bitcast.136), kind=kOutput, calls=%fused_computation.54 | convolution fusion | flops 1611005952 | bytes 6553600 | tf_op jit(solution)/shard_map/dot_general | solution.py:190
  164.4 14.1 %reshape.218 = bf16[2,17,128,1024]{3,2,1,0:T(8,128)(2,1)} reshape(bf16[2,1088,2,1024]{3,2,1,0:T(2,128)(2,1)} %copy.89) | data formatting | bytes 17825792 | tf_op jit(solution)/shard_map/reshape | solution.py:64
  178.5 10.1 %convert_bitcast_fusion = bf16[2,17,128,1024]{3,2,1,0:T(8,128)(2,1)} fusion(bf16[2,17,128,1024]{3,2,1,0:T(8,128)(2,1)} %reshape.218, s32[128]{0:T(128)S(1)} %fusion.82), kind=kOutput, calls=%fused_computation.6 | convolution fusion | flops 1145323520 | bytes 17826304 | tf_op jit(solution)/shard_map/ks,rbsd->rbkd/dot_general | solution.py:69
  188.6 9.1 %fusion.88 = (bf16[2,17,64,1024]{3,2,1,0:T(8,128)(2,1)}, bf16[2,17,64,1024]{3,2,1,0:T(8,128)(2,1)}) fusion(bf16[2,17,128,1024]{3,2,1,0:T(8,128)(2,1)} %convert_bitcast_fusion), kind=kLoop, calls=%fused_computation.137 | loop fusion | bytes 17825792 | tf_op jit(solution)/shard_map/slice | solution.py:73
  197.8 2.3 copy-done
  200.0 2.3 copy-done.2
  202.3 16.9 %shard_map.78 = (bf16[2,192,1024]{2,1,0:T(8,128)(2,1)S(1)}, f32[2,192,128]{2,1,0:T(8,128)S(1)}) custom-call(s32[3]{0:T(128)S(1)} %pad_add_fusion.1.info, f32[8]{0:T(128)S(1)} %multiply_exponential_fusion.slopes, bf16[2,192,1024]{2,1,0:T(8,128)(2,1)S(1)} %bitcast.126, bf16[2,1088,1024]{2,1,0:T(8,128)(2,1)S(1)} %bitcast.124, ...), custom_call_target="tpu_custom_call" | custom-call | flops 2013265920 | bytes 12058624 | tf_op jit(solution)/shard_map/pallas_call | solution.py:119
  219.2 1.5 collective-permute-start.10
  220.7 0.5 collective-permute-start.9
  221.3 1.5 collective-permute-start.1
  222.8 23.0 %collective-permute-done.9 = f32[2,192,8]{2,1,0:T(8,128)S(1)} collective-permute-done((f32[2,192,8]{2,1,0:T(8,128)S(1)}, f32[2,192,8]{2,1,0:T(8,128)S(1)}, u32[]{:S(2)}, u32[]{:S(2)}) %collective-permute-start.9) | collective-permute-done | bytes 12320 | tf_op jit(solution)/shard_map/ppermute | solution.py:19
  245.8 0.5 mul.157
  246.3 0.5 mul.154
  246.8 3.4 convolution_convert_fusion
  250.4 0.6 fusion.91
  252.3 9.9 %copy.28 = bf16[2,1088,2,1024]{3,1,0,2:T(8,128)(2,1)} copy(bf16[2,1088,2,1024]{3,2,1,0:T(2,128)(2,1)} %copy.89) | data formatting | bytes 17825792 | tf_op jit(solution)/shard_map/optimization_barrier | solution.py:192
  262.6 2.3 copy-done.1
  264.8 2.3 copy-done.3
  267.1 16.9 %shard_map.77 = (bf16[2,192,1024]{2,1,0:T(8,128)(2,1)S(1)}, f32[2,192,128]{2,1,0:T(8,128)S(1)}) custom-call(s32[3]{0:T(128)S(1)} %pad_add_fusion.1.info, f32[8]{0:T(128)S(1)} %multiply_exponential_fusion.slopes, bf16[2,192,1024]{2,1,0:T(8,128)(2,1)S(1)} %bitcast.127, bf16[2,1088,1024]{2,1,0:T(8,128)(2,1)S(1)} %bitcast.125, ...), custom_call_target="tpu_custom_call" | custom-call | flops 2013265920 | bytes 12058624 | tf_op jit(solution)/shard_map/pallas_call | solution.py:119
  284.5 1.6 collective-permute-start.7
  286.1 8.2 %fusion.87 = (bf16[1,1088,2,1024]{3,1,0,2:T(8,128)(2,1)}, bf16[1,1088,2,1024]{3,1,0,2:T(8,128)(2,1)}) fusion(bf16[2,1088,2,1024]{3,1,0,2:T(8,128)(2,1)} %copy.28), kind=kLoop, calls=%fused_computation.136 | loop fusion | bytes 17825792 | tf_op jit(solution)/shard_map/slice | solution.py:226
  294.4 12.5 %collective-permute-done.7 = bf16[2,192,1024]{2,1,0:T(8,128)(2,1)S(1)} collective-permute-done((bf16[2,192,1024]{2,1,0:T(8,128)(2,1)S(1)}, bf16[2,192,1024]{2,1,0:T(8,128)(2,1)S(1)}, u32[]{:S(2)}, u32[]{:S(2)}) %collective-permute-start.7) | collective-permute-done | bytes 786464 | tf_op jit(solution)/shard_map/ppermute | solution.py:19
  306.9 0.5 mul.151
  307.3 0.5 mul.148
  307.8 3.4 convolution_convert_fusion.1
  311.3 2.7 copy.27
  314.0 1.6 copy.26
  315.9 1.5 fusion.3
  317.4 4.8 %fusion.86 = (bf16[1,1152,2,1024]{3,1,0,2:T(8,128)(2,1)}, bf16[1,1152,2,1024]{3,1,0,2:T(8,128)(2,1)}) fusion(bf16[2,1152,2,1024]{3,1,0,2:T(8,128)(2,1)S(1)} %fusion.3), kind=kLoop, calls=%fused_computation.135 | loop fusion | bytes 18874368 | tf_op jit(solution)/shard_map/slice | solution.py:222
  322.2 2.9 dynamic-slice_select_fusion.1
  325.1 2.9 dynamic-slice_select_fusion
  328.1 2.8 copy_dynamic-update-slice_fusion.1
  330.8 2.8 copy_dynamic-update-slice_fusion
  333.6 13.2 %reduce-scatter.3.cloned.1.call-done = bf16[96,2048]{1,0:T(8,128)(2,1)} async-done(((bf16[384,2048]{1,0:T(8,128)(2,1)}), bf16[96,2048]{1,0:T(8,128)(2,1)}) %reduce-scatter.3.cloned.1.call-update) | async-done | bytes 393232 | tf_op jit(solution)/shard_map/reduce_scatter | solution.py:248
  346.9 2.3 fusion.29
  (74 shorter events, 4.3 us)
Async XLA Ops:
  7.2 8.6 %copy-start.6 = (bf16[192,2048]{1,0:T(8,128)(2,1)S(1)}, bf16[192,2048]{1,0:T(8,128)(2,1)}, u32[]{:S(2)}) copy-start(bf16[192,2048]{1,0:T(8,128)(2,1)} %param.6) | copy-start | bytes 2359300
  7.2 49.7 %all-gather.11.cloned.1.call-start = ((), (), s32[]{:S(2)}) async-start(), calls=%async_computation.4 | async-start | bytes 1966080 | tf_op jit(solution)/shard_map/all_gather | solution.py:157
  16.8 77.6 %all-gather.13.cloned.1.call-start = ((), (), s32[]{:S(2)}) async-start(), calls=%async_computation.5 | async-start | bytes 1966080 | tf_op jit(solution)/shard_map/all_gather | solution.py:157
  17.5 293.8 %all-gather.17.cloned.1.call-start = ((), (), s32[]{:S(2)}) async-start(), calls=%async_computation.7 | async-start | bytes 2359296 | tf_op jit(solution)/shard_map/all_gather | solution.py:206
  18.0 12.6 %collective-permute-start = (f32[2,192]{1,0:T(2,128)S(1)}, f32[2,192]{1,0:T(2,128)S(1)}, u32[]{:S(2)}, u32[]{:S(2)}) collective-permute-start(f32[2,192]{1,0:T(2,128)S(1)} %pad_maximum_fusion.2), channel_id=1, source_target_pairs={{0,1},{1,0},{2,3},{3,2},{4,5},{5,4},{6,7},{7,6},{8,9},{9,8},{10,11... | collective-permute-start | bytes 4616 | tf_op jit(solution)/shard_map/ppermute | solution.py:19
  21.3 9.2 %copy-start.14 = (s32[2]{0:T(128)S(1)}, s32[2]{0:T(128)}, u32[]{:S(2)}) copy-start(s32[2]{0:T(128)} %param.11) | copy-start | bytes 28
  21.3 73.1 %copy-start.13 = (f32[2048]{0:T(1024)S(1)}, f32[2048]{0:T(1024)}, u32[]{:S(2)}) copy-start(f32[2048]{0:T(1024)} %param.7) | copy-start | bytes 24580
  94.4 3.1 copy-start.11
  97.4 5.9 %copy-start.12 = (bf16[4,96,2048]{2,1,0:T(8,128)(2,1)}, bf16[4,96,2048]{2,1,0:T(8,128)(2,1)S(1)}, u32[]{:S(2)}) copy-start(bf16[4,96,2048]{2,1,0:T(8,128)(2,1)S(1)} %get-tuple-element.37) | copy-start | bytes 4718596
  99.3 2.2 copy-start.10
  105.1 5.9 %copy-start.9 = (bf16[2048,8,128]{2,1,0:T(8,128)(2,1)S(1)}, bf16[2048,8,128]{2,1,0:T(8,128)(2,1)}, u32[]{:S(2)}) copy-start(bf16[2048,8,128]{2,1,0:T(8,128)(2,1)} %get-tuple-element.22) | copy-start | bytes 12582916
  105.2 12.1 %collective-permute-start.3 = (bf16[2,96,1024]{2,1,0:T(8,128)(2,1)S(1)}, bf16[2,96,1024]{2,1,0:T(8,128)(2,1)S(1)}, u32[]{:S(2)}, u32[]{:S(2)}) collective-permute-start(bf16[2,96,1024]{2,1,0:T(8,128)(2,1)S(1)} %broadcast_select_fusion.2), channel_id=1, source_target_pairs={{0,1},{1,0},{2,3},{3,2},{4,5},{5,4},{6,7},{7,6},{8,9},{9,8},{10,11... | collective-permute-start | bytes 1179656 | tf_op jit(solution)/shard_map/ppermute | solution.py:19
  106.8 18.9 %collective-permute-start.2 = (bf16[2,96,1024]{2,1,0:T(8,128)(2,1)S(1)}, bf16[2,96,1024]{2,1,0:T(8,128)(2,1)S(1)}, u32[]{:S(2)}, u32[]{:S(2)}) collective-permute-start(bf16[2,96,1024]{2,1,0:T(8,128)(2,1)S(1)} %broadcast_select_fusion.3), channel_id=1, source_target_pairs={{0,1},{1,0},{2,3},{3,2},{4,5},{5,4},{6,7},{7,6},{8,9},{9,8},{10,11... | collective-permute-start | bytes 1179656 | tf_op jit(solution)/shard_map/ppermute | solution.py:19
  108.2 25.9 %collective-permute-start.5 = (bf16[2,96,1024]{2,1,0:T(8,128)(2,1)}, bf16[2,96,1024]{2,1,0:T(8,128)(2,1)S(1)}, u32[]{:S(2)}, u32[]{:S(2)}) collective-permute-start(bf16[2,96,1024]{2,1,0:T(8,128)(2,1)} %broadcast_select_fusion), channel_id=1, source_target_pairs={{0,1},{1,0},{2,3},{3,2},{4,5},{5,4},{6,7},{7,6},{8,9},{9,8},{10,11... | collective-permute-start | bytes 1179656 | tf_op jit(solution)/shard_map/ppermute | solution.py:19
  110.5 32.1 %collective-permute-start.4 = (bf16[2,96,1024]{2,1,0:T(8,128)(2,1)}, bf16[2,96,1024]{2,1,0:T(8,128)(2,1)S(1)}, u32[]{:S(2)}, u32[]{:S(2)}) collective-permute-start(bf16[2,96,1024]{2,1,0:T(8,128)(2,1)} %broadcast_select_fusion.1), channel_id=1, source_target_pairs={{0,1},{1,0},{2,3},{3,2},{4,5},{5,4},{6,7},{7,6},{8,9},{9,8},{10,11... | collective-permute-start | bytes 1179656 | tf_op jit(solution)/shard_map/ppermute | solution.py:19
  112.8 45.4 %collective-permute-start.8 = (bf16[384,1024]{1,0:T(8,128)(2,1)S(1)}, bf16[384,1024]{1,0:T(8,128)(2,1)}, u32[]{:S(2)}, u32[]{:S(2)}) collective-permute-start(bf16[384,1024]{1,0:T(8,128)(2,1)S(1)} %fusion.37), channel_id=1, source_target_pairs={{0,1},{1,0},{2,3},{3,2},{4,5},{5,4},{6,7},{7,6},{8,9},{9,8},{10,11... | collective-permute-start | bytes 2359304 | tf_op jit(solution)/shard_map/ppermute | solution.py:19
  159.7 154.3 %all-gather.15.cloned.1.call-start = ((), (), s32[]{:S(2)}) async-start(), calls=%async_computation.6 | async-start | bytes 2359296 | tf_op jit(solution)/shard_map/all_gather | solution.py:206
  188.5 9.2 %copy-start.4 = (bf16[2,192,1024]{2,1,0:T(8,128)(2,1)S(1)}, bf16[2,192,1024]{2,1,0:T(8,128)(2,1)}, u32[]{:S(2)}) copy-start(bf16[2,192,1024]{2,1,0:T(8,128)(2,1)} %pad_maximum_fusion.nk_ref) | copy-start | bytes 2359300
  188.5 9.2 %copy-start.5 = (bf16[2,192,1024]{2,1,0:T(8,128)(2,1)S(1)}, bf16[2,192,1024]{2,1,0:T(8,128)(2,1)}, u32[]{:S(2)}) copy-start(bf16[2,192,1024]{2,1,0:T(8,128)(2,1)} %pad_maximum_fusion.1.nv_ref) | copy-start | bytes 2359300
  197.7 135.9 %reduce-scatter.5.cloned.1.call-start = ((), (), s32[]{:S(2)}) async-start(), calls=%async_computation.3 | async-start | bytes 1966080 | tf_op jit(solution)/shard_map/reduce_scatter | solution.py:248
  197.8 2.3 copy-start
  200.0 2.3 copy-start.2
  219.2 27.6 %copy-start.15 = (bf16[1024,2048]{1,0:T(8,128)(2,1)S(1)}, bf16[1024,2048]{1,0:T(8,128)(2,1)}, u32[]{:S(2)}) copy-start(bf16[1024,2048]{1,0:T(8,128)(2,1)} %param.9) | copy-start | bytes 12582916
  219.2 26.6 %collective-permute-start.10 = (bf16[2,192,1024]{2,1,0:T(8,128)(2,1)S(1)}, bf16[2,192,1024]{2,1,0:T(8,128)(2,1)S(1)}, u32[]{:S(2)}, u32[]{:S(2)}) collective-permute-start(bf16[2,192,1024]{2,1,0:T(8,128)(2,1)S(1)} %get-tuple-element.16), channel_id=1, source_target_pairs={{0,1},{1,0},{2,3},{3,2},{4,5},{5,4},{6,7},{7,6},{8,9},{9,8},{10,11... | collective-permute-start | bytes 2359304 | tf_op jit(solution)/shard_map/ppermute | solution.py:19
  220.7 25.0 %collective-permute-start.9 = (f32[2,192,8]{2,1,0:T(8,128)S(1)}, f32[2,192,8]{2,1,0:T(8,128)S(1)}, u32[]{:S(2)}, u32[]{:S(2)}) collective-permute-start(f32[2,192,8]{2,1,0:T(8,128)S(1)} %bitcast.129), channel_id=1, source_target_pairs={{0,1},{1,0},{2,3},{3,2},{4,5},{5,4},{6,7},{7,6},{8,9},{9,8},{10,11... | collective-permute-start | bytes 36872 | tf_op jit(solution)/shard_map/ppermute | solution.py:19
  221.3 41.0 %collective-permute-start.1 = (bf16[384,1024]{1,0:T(8,128)(2,1)S(1)}, bf16[384,1024]{1,0:T(8,128)(2,1)S(1)}, u32[]{:S(2)}, u32[]{:S(2)}) collective-permute-start(bf16[384,1024]{1,0:T(8,128)(2,1)S(1)} %fusion.34), channel_id=1, source_target_pairs={{0,1},{1,0},{2,3},{3,2},{4,5},{5,4},{6,7},{7,6},{8,9},{9,8},{10,11... | collective-permute-start | bytes 2359304 | tf_op jit(solution)/shard_map/ppermute | solution.py:19
  250.2 96.7 %reduce-scatter.3.cloned.1.call-start = ((), (), s32[]{:S(2)}) async-start(), calls=%async_computation.2 | async-start | bytes 1966080 | tf_op jit(solution)/shard_map/reduce_scatter | solution.py:248
  262.6 2.3 copy-start.1
  264.8 2.3 copy-start.3
  284.0 10.3 %collective-permute-start.6 = (f32[2,192,8]{2,1,0:T(8,128)S(1)}, f32[2,192,8]{2,1,0:T(8,128)S(1)}, u32[]{:S(2)}, u32[]{:S(2)}) collective-permute-start(f32[2,192,8]{2,1,0:T(8,128)S(1)} %bitcast.128), channel_id=1, source_target_pairs={{0,1},{1,0},{2,3},{3,2},{4,5},{5,4},{6,7},{7,6},{8,9},{9,8},{10,11... | collective-permute-start | bytes 36872 | tf_op jit(solution)/shard_map/ppermute | solution.py:19
  284.5 22.4 %collective-permute-start.7 = (bf16[2,192,1024]{2,1,0:T(8,128)(2,1)S(1)}, bf16[2,192,1024]{2,1,0:T(8,128)(2,1)S(1)}, u32[]{:S(2)}, u32[]{:S(2)}) collective-permute-start(bf16[2,192,1024]{2,1,0:T(8,128)(2,1)S(1)} %get-tuple-element.13), channel_id=1, source_target_pairs={{0,1},{1,0},{2,3},{3,2},{4,5},{5,4},{6,7},{7,6},{8,9},{9,8},{10,11... | collective-permute-start | bytes 2359304 | tf_op jit(solution)/shard_map/ppermute | solution.py:19
  294.3 13.5 %copy-start.16 = (bf16[1024,2048]{1,0:T(8,128)(2,1)S(1)}, bf16[1024,2048]{1,0:T(8,128)(2,1)}, u32[]{:S(2)}) copy-start(bf16[1024,2048]{1,0:T(8,128)(2,1)} %param.9) | copy-start | bytes 12582916
  314.0 1.9 copy-start.8
  328.1 18.8 %copy-start.7 = (bf16[192,2048]{1,0:T(8,128)(2,1)S(1)}, bf16[192,2048]{1,0:T(8,128)(2,1)}, u32[]{:S(2)}) copy-start(bf16[192,2048]{1,0:T(8,128)(2,1)} %param.6) | copy-start | bytes 2359300
Sparse Core Ops, SparseCore 0:
  16.9 39.9 all-gather.10
  58.4 35.9 all-gather.12
  159.8 26.3 all-gather.16
  197.8 29.1 all-gather.14
  250.3 35.2 reduce-scatter.4
  311.4 35.4 reduce-scatter.2

commit v3 on v2

--- a/solution.py
+++ b/solution.py
@@ -56,6 +56,25 @@
     totals = lax.psum(factor, "gy")
     accums = lax.psum((part.astype(jnp.float32) * factor[..., None]).astype(jnp.bfloat16), "gy")
     return (accums.astype(jnp.float32) / totals[..., None]).astype(jnp.bfloat16)
+
+
+def copy_kernel(source, after, target, sem):
+    copy = pltpu.make_async_copy(source, target, sem)
+    copy.start()
+    copy.wait()
+
+
+def copy_after(source, after):
+    return pl.pallas_call(
+        copy_kernel,
+        out_shape=jax.ShapeDtypeStruct(source.shape, source.dtype),
+        in_specs=[pl.BlockSpec(memory_space=pl.ANY)] * 2,
+        out_specs=pl.BlockSpec(memory_space=pl.ANY),
+        scratch_shapes=[pltpu.SemaphoreType.DMA],
+        cost_estimate=pl.CostEstimate(
+            flops=0, bytes_accessed=4 * source.size, transcendentals=0
+        ),
+    )(source, after)
 
 
 def split_cache(cache):
@@ -160,6 +179,8 @@
     mean = sums[0] / D
     rstd = lax.rsqrt(sums[1] / D - mean * mean + norm_eps)
     stats = lax.all_gather(jnp.stack([mean, rstd]), "gx", axis=0)
+    stats, split_from = lax.optimization_barrier((stats, kv_cache))
+    old_keys, old_values = split_cache(split_from)
 
     depth, local_heads = w_qkv.shape[:2]
     head_size = w_qkv.shape[2] // 3
@@ -188,12 +209,16 @@
             for w in (w_k, w_v)
         ]
         q = jnp.dot(normed, w_q, preferred_element_type=jnp.float32).astype(jnp.bfloat16)
-        if c == 0:
-            q, kv_cache = lax.optimization_barrier((q, kv_cache))
+        last = q
         keys.append(scatter_gy(kv[0]))
         values.append(scatter_gy(kv[1]))
         queries.append(sum_gy(q).reshape(requests, rows, width))
-    old_keys, old_values = split_cache(kv_cache)
+        if c + 1 < CHUNKS:
+            keys, values, queries, old_keys, old_values, gathered[c + 1] = (
+                lax.optimization_barrier(
+                    (keys, values, queries, old_keys, old_values, gathered[c + 1])
+                )
+            )
 
     flat = jnp.arange(rows, dtype=jnp.int32)
     tokens = [(flat // piece) * local_rows + c * piece + flat % piece for c in range(CHUNKS)]
@@ -208,24 +233,21 @@
         full = full.reshape(requests, CHUNKS, share, piece, width).transpose(0, 2, 1, 3, 4)
         return full.reshape(requests, group, width)
 
-    sent_keys, sent_values, queries[-1] = lax.optimization_barrier(
-        (own_keys, own_values, queries[-1])
-    )
+    sent_keys, sent_values, queries = lax.optimization_barrier((own_keys, own_values, queries))
     fresh = jnp.stack([whole(sent_keys), whole(sent_values)], axis=2)
     window = min(group, block)
     padded = jnp.pad(fresh, ((0, 0), (window, window), (0, 0), (0, 0)))
-    updated = kv_cache
+    updated = copy_after(kv_cache, last)
     for r in range(requests):
         away = cache_len[r] - gy * block
         begin = jnp.clip(away, 0, block - window)
-        taken = lax.dynamic_slice_in_dim(
-            padded[r], jnp.clip(window + begin - away, 0, group + window), window
-        )
+        start = jnp.clip(window + begin - away, 0, group + window)
+        taken = lax.dynamic_slice(padded, (r, start, 0, 0), (1, window, 2, width))
         offset = begin - away + jnp.arange(window, dtype=jnp.int32)
         inside = (offset >= 0) & (offset < group)
-        old = lax.dynamic_slice_in_dim(kv_cache[r], begin, window)
-        new = jnp.where(inside[:, None, None], taken, old)
-        updated = lax.dynamic_update_slice(updated, new[None], (r, begin, 0, 0))
+        old = lax.dynamic_slice(kv_cache, (r, begin, 0, 0), (1, window, 2, width))
+        new = jnp.where(inside[None, :, None, None], taken, old)
+        updated = lax.dynamic_update_slice(updated, new, (r, begin, 0, 0))
 
     head_ids = lax.axis_index("gx") * local_heads + jnp.arange(local_heads, dtype=jnp.int32)
     slopes = jnp.exp2(-8.0 * (head_ids + 1).astype(jnp.float32) / (local_heads * gx_n))

time: 357 us -> 583 us (1.63)
  Pallas kernels: 33.8 us -> 305 us
  waiting for transfers between devices: 142 us -> 76.4 us
  other arithmetic: 19.7 us -> 73.7 us
  local copies, waits for them, and re-layouts: 87.2 us -> 50.8 us
    pallas_call x0 -> x1, Pallas kernels: none -> 271 us  [copy_after(): pl.pallas_call(copy_kernel, out_shape=jax.ShapeDtypeStruct(source.shape,...]
    all_gather x2, waiting for transfers between devices: 51.3 us -> 0.02 us  [shards(): lax.all_gather(hidden[c * piece:(c + 1) * piece], 'gx', axis=0)]
    another operation x1, other arithmetic: 1.52 us -> 45.4 us  [shards(): fresh = jnp.stack([whole(sent_keys), whole(sent_values)], axis=2)]
    optimization_barrier x2 -> x0, local copies, waits for them, and re-layouts: 18.5 us -> none  [shards(): q, kv_cache = lax.optimization_barrier((q, kv_cache))]
    reduce_scatter x2, waiting for transfers between devices: 13.2 us -> 0.01 us  [shards(): lax.psum_scatter(jnp.dot(attn, w_out, preferred_element_type=jnp.float32)...]
    slice x2 -> x0, local copies, waits for them, and re-layouts: 13 us -> none  [the longest x1 8.16 us: shards(): old = lax.dynamic_slice_in_dim(kv_cache[r], begin, window)]
    dynamic_update_slice x0 -> x2, other arithmetic: none -> 9.49 us  [shards(): updated = lax.dynamic_update_slice(updated, new, (r, begin, 0, 0))]
  transfers between devices with their start and end apart: 17 -> 17, of which waited for: 10 -> 6; matrix products, arithmetic and copies ran while one was open for 29% -> 23% of each run, Pallas kernels for 9% -> 52%
where the time goes in v3:
time: 583 us; the launch traced here: 582 us
  Pallas kernels  305 us (52%)
  waiting for transfers between devices  76.4 us (13%)
  other arithmetic  73.7 us (13%)
  local copies, waits for them, and re-layouts  50.8 us (9%)
  matrix products  34.5 us (6%)
  between operations  15.9 us (3%)
  starting transfers between devices  12.8 us (2%)
  blocking collectives  12.5 us (2%)
    pallas_call x1, Pallas kernels, copy_after(): pl.pallas_call(copy_kernel, out_shape=jax.ShapeDtypeStruct(source.shape,...  271 us
    ppermute x11, waiting for transfers between devices, other(): return lax.ppermute(value, 'gy', [(0, 1), (1, 0)])  76.1 us
    another operation x1, other arithmetic, shards(): fresh = jnp.stack([whole(sent_keys), whole(sent_values)], axis=2)  45.4 us
    pallas_call x2, Pallas kernels, attend(): pl.pallas_call(functools.partial(attend_kernel, 1.0 / math.sqrt(size)), g...  34.2 us
    reshape x1, local copies, waits for them, and re-layouts, split_cache(): rows = cache.reshape(requests, 2 * block // size, size, width)  14 us
    all_gather x1, blocking collectives, shards(): stats = lax.all_gather(jnp.stack([mean, rstd]), 'gx', axis=0)  12.5 us
    ppermute x11, starting transfers between devices, other(): return lax.ppermute(value, 'gy', [(0, 1), (1, 0)])  12.5 us
  transfers between devices with their start and end apart: 17, of which 6 were waited for; matrix products, arithmetic and copies ran while one was open for 23% of the time, Pallas kernels for 52%

profile of v3, /device:TPU:0, one launch (start us, length us, event | category | flops | bytes accessed | tf_op | source)
XLA Modules:
  0.0 581.9 jit_solution(6144531334602173918)
XLA Ops:
  7.2 2.1 fusion.82
  9.4 1.5 convert_reduce_fusion
  10.9 3.0 collective-permute-start
  14.0 9.1 %fusion.80 = (bf16[2048,8,128]{2,1,0:T(8,128)(2,1)}, bf16[2048,8,128]{2,1,0:T(8,128)(2,1)}, bf16[2048,8,128]{2,1,0:T(8,128)(2,1)}) fusion(bf16[2048,8,384]{2,1,0:T(8,128)(2,1)} %param.8), kind=kLoop, calls=%fused_computation.127 | loop fusion | bytes 25165824 | tf_op jit(solution)/shard_map/slice | solution.py:188
  23.2 12.5 %all-gather.5 = f32[4,2,192]{2,1,0:T(2,128)S(1)} all-gather(f32[1,2,192]{2,1,0:T(2,128)S(1)} %maximum_bitcast_fusion), channel_id=3, replica_groups=mesh['req'=4,'gx'=4,'gy'=2] {'gx'}, dimensions={0}, use_global_device_ids=true | all-gather | bytes 7680 | tf_op jit(solution)/shard_map/all_gather | solution.py:181
  35.8 14.0 %reshape.222 = bf16[2,17,128,1024]{3,2,1,0:T(8,128)(2,1)} reshape(bf16[2,1088,2,1024]{3,2,1,0:T(2,128)(2,1)} %source.1) | data formatting | bytes 17825792 | tf_op jit(solution)/shard_map/reshape | solution.py:83
  49.8 10.1 %convert_bitcast_fusion = bf16[2,17,128,1024]{3,2,1,0:T(8,128)(2,1)} fusion(bf16[2,17,128,1024]{3,2,1,0:T(8,128)(2,1)} %reshape.222, s32[128]{0:T(128)S(1)} %fusion.77), kind=kOutput, calls=%fused_computation.2 | convolution fusion | flops 1145323520 | bytes 17826304 | tf_op jit(solution)/shard_map/ks,rbsd->rbkd/dot_general | solution.py:88
  59.9 1.9 fusion.20
  61.8 4.1 fusion.29
  66.0 1.8 fusion.35
  67.8 0.5 collective-permute-start.2
  68.3 0.8 broadcast_select_fusion.5
  69.1 1.6 collective-permute-start.1
  70.7 2.7 fusion.41
  73.4 0.4 collective-permute-start.3
  73.8 4.7 fusion.81
  78.5 1.6 collective-permute-done.2
  80.1 1.2 add_convert_fusion.4
  81.3 7.1 %collective-permute-done.1 = bf16[2,96,1024]{2,1,0:T(8,128)(2,1)S(1)} collective-permute-done((bf16[2,96,1024]{2,1,0:T(8,128)(2,1)}, bf16[2,96,1024]{2,1,0:T(8,128)(2,1)S(1)}, u32[]{:S(2)}, u32[]{:S(2)}) %collective-permute-start.1) | collective-permute-done | bytes 393248 | tf_op jit(solution)/shard_map/ppermute | solution.py:19
  88.4 1.0 add_convert_fusion.5
  89.4 12.2 %collective-permute-done.3 = bf16[384,1024]{1,0:T(8,128)(2,1)} collective-permute-done((bf16[384,1024]{1,0:T(8,128)(2,1)}, bf16[384,1024]{1,0:T(8,128)(2,1)}, u32[]{:S(2)}, u32[]{:S(2)}) %collective-permute-start.3) | collective-permute-done | bytes 786464 | tf_op jit(solution)/shard_map/ppermute | solution.py:19
  101.5 1.7 add_convert_fusion.1
  103.2 1.9 multiply_convert_fusion
  105.2 4.1 fusion.44.after
  109.4 2.0 fusion.32
  111.4 0.7 collective-permute-start.4
  112.1 1.8 fusion.38
  113.9 1.4 collective-permute-start.6
  115.3 0.8 broadcast_select_fusion.2
  116.1 0.7 collective-permute-start.5
  116.8 6.7 %collective-permute-done.4 = bf16[2,96,1024]{2,1,0:T(8,128)(2,1)S(1)} collective-permute-done((bf16[2,96,1024]{2,1,0:T(8,128)(2,1)S(1)}, bf16[2,96,1024]{2,1,0:T(8,128)(2,1)S(1)}, u32[]{:S(2)}, u32[]{:S(2)}) %collective-permute-start.4) | collective-permute-done | bytes 393248 | tf_op jit(solution)/shard_map/ppermute | solution.py:19
  123.7 1.0 pad_maximum_fusion.nk_ref
  124.7 19.5 %collective-permute-done.5 = bf16[2,96,1024]{2,1,0:T(8,128)(2,1)} collective-permute-done((bf16[2,96,1024]{2,1,0:T(8,128)(2,1)}, bf16[2,96,1024]{2,1,0:T(8,128)(2,1)}, u32[]{:S(2)}, u32[]{:S(2)}) %collective-permute-start.5) | collective-permute-done | bytes 393248 | tf_op jit(solution)/shard_map/ppermute | solution.py:19
  144.2 1.2 add_convert_fusion.2
  145.4 0.9 pad_maximum_fusion.1.nv_ref
  146.3 1.7 add_convert_fusion
  148.8 2.3 copy-done
  151.0 2.3 copy-done.2
  153.3 16.9 %shard_map.77 = (bf16[2,192,1024]{2,1,0:T(8,128)(2,1)S(1)}, f32[2,192,128]{2,1,0:T(8,128)S(1)}) custom-call(s32[3]{0:T(128)S(1)} %pad_add_fusion.1.info, f32[8]{0:T(128)S(1)} %multiply_exponential_fusion.slopes, bf16[2,192,1024]{2,1,0:T(8,128)(2,1)S(1)} %bitcast.125, bf16[2,1088,1024]{2,1,0:T(8,128)(2,1)S(1)} %bitcast.123, ...), custom_call_target="tpu_custom_call" | custom-call | flops 2013265920 | bytes 12058624 | tf_op jit(solution)/shard_map/pallas_call | solution.py:138
  170.2 1.0 collective-permute-start.8
  171.1 1.1 collective-permute-start.7
  172.3 29.0 %collective-permute-done.7 = f32[2,192,8]{2,1,0:T(8,128)S(1)} collective-permute-done((f32[2,192,8]{2,1,0:T(8,128)S(1)}, f32[2,192,8]{2,1,0:T(8,128)S(1)}, u32[]{:S(2)}, u32[]{:S(2)}) %collective-permute-start.7) | collective-permute-done | bytes 12320 | tf_op jit(solution)/shard_map/ppermute | solution.py:19
  201.4 0.5 mul.148
  201.9 0.5 mul.151
  202.3 3.5 convolution_convert_fusion.1
  206.0 2.3 copy-done.1
  208.2 2.3 copy-done.3
  210.5 17.4 %shard_map.78 = (bf16[2,192,1024]{2,1,0:T(8,128)(2,1)}, f32[2,192,128]{2,1,0:T(8,128)S(1)}) custom-call(s32[3]{0:T(128)S(1)} %pad_add_fusion.1.info, f32[8]{0:T(128)S(1)} %multiply_exponential_fusion.slopes, bf16[2,192,1024]{2,1,0:T(8,128)(2,1)S(1)} %bitcast.126, bf16[2,1088,1024]{2,1,0:T(8,128)(2,1)S(1)} %bitcast.124, bf16[2,1088,1024]{2,1,0:T(8,128)(2,1)S(1)} %bitcast.122, ...), custom_call_target="tpu_custom_call" | custom-call | flops 2013265920 | bytes 12058624 | tf_op jit(solution)/shard_map/pallas_call | solution.py:138
  227.8 0.2 collective-permute-start.10
  228.1 0.6 fusion.84
  230.0 1.9 collective-permute-start.9
  231.8 271.1 %shard_map.79 = bf16[2,1088,2,1024]{3,2,1,0:T(2,128)(2,1)} custom-call(bf16[2,1088,2,1024]{3,2,1,0:T(2,128)(2,1)} %source.1, bf16[384,1024]{1,0:T(8,128)(2,1)} %copy-done.11), custom_call_target="tpu_custom_call" | custom-call | bytes 17825792 | tf_op jit(solution)/shard_map/pallas_call | solution.py:68
  503.1 0.5 mul.154
  503.5 0.5 mul.157
  504.0 1.1 copy-done.16
  505.1 4.6 convolution_convert_fusion
  509.7 1.6 copy.20
  511.4 1.6 copy.21
  513.0 2.4 copy.23
  515.4 2.4 copy.22
  517.8 45.4 %select_maximum_fusion = bf16[2,1152,2,1024]{3,2,1,0:T(2,128)(2,1)S(1)} fusion(bf16[2,384,1,1024]{3,2,1,0:T(2,128)(2,1)S(1)} %copy.23, bf16[2,384,1,1024]{3,2,1,0:T(2,128)(2,1)S(1)} %copy.22), kind=kLoop, calls=%fused_computation.1 | loop fusion | flops 42467328 | bytes 12582912 | tf_op jit(solution)/shard_map/stack | solution.py:237
  563.3 4.7 fusion.21
  568.0 4.8 fusion.22
  572.8 2.3 fusion.24
  (80 shorter events, 1.6 us)
Async XLA Ops:
  7.2 52.7 %all-gather.11.cloned.1.call-start = ((), (), s32[]{:S(2)}) async-start(), calls=%async_computation.4 | async-start | bytes 1966080 | tf_op jit(solution)/shard_map/all_gather | solution.py:176
  9.3 93.9 %all-gather.13.cloned.1.call-start = ((), (), s32[]{:S(2)}) async-start(), calls=%async_computation.5 | async-start | bytes 1966080 | tf_op jit(solution)/shard_map/all_gather | solution.py:176
  10.9 12.3 %collective-permute-start = (f32[2,192]{1,0:T(2,128)S(1)}, f32[2,192]{1,0:T(2,128)S(1)}, u32[]{:S(2)}, u32[]{:S(2)}) collective-permute-start(f32[2,192]{1,0:T(2,128)S(1)} %pad_maximum_fusion.2), channel_id=1, source_target_pairs={{0,1},{1,0},{2,3},{3,2},{4,5},{5,4},{6,7},{7,6},{8,9},{9,8},{10,11... | collective-permute-start | bytes 4616 | tf_op jit(solution)/shard_map/ppermute | solution.py:19
  13.9 495.8 %all-gather.15.cloned.1.call-start = ((), (), s32[]{:S(2)}) async-start(), calls=%async_computation.6 | async-start | bytes 2359296 | tf_op jit(solution)/shard_map/all_gather | solution.py:231
  49.8 10.1 %copy-start.13 = (f32[2048]{0:T(1024)S(1)}, f32[2048]{0:T(1024)}, u32[]{:S(2)}) copy-start(f32[2048]{0:T(1024)} %param.7) | copy-start | bytes 24580
  61.8 4.1 copy-start.7
  66.0 4.8 copy-start.10
  66.0 7.9 %slice-start = ((s8[8912896]{0:T(1024)(128)(4,1)}), s8[4194304]{0:T(1024)(128)(4,1)S(1)}, s32[]{:S(2)}) async-start(s8[8912896]{0:T(1024)(128)(4,1)} %bitcast.132), calls=%async_computation.8 | async-start | bytes 8388608
  66.0 7.9 %slice-start.1 = ((s8[8912896]{0:T(1024)(128)(4,1)}), s8[4194304]{0:T(1024)(128)(4,1)S(1)}, s32[]{:S(2)}) async-start(s8[8912896]{0:T(1024)(128)(4,1)} %bitcast.132), calls=%async_computation.9 | async-start | bytes 8388608
  67.8 12.2 %collective-permute-start.2 = (bf16[2,96,1024]{2,1,0:T(8,128)(2,1)S(1)}, bf16[2,96,1024]{2,1,0:T(8,128)(2,1)}, u32[]{:S(2)}, u32[]{:S(2)}) collective-permute-start(bf16[2,96,1024]{2,1,0:T(8,128)(2,1)S(1)} %broadcast_select_fusion.4), channel_id=1, source_target_pairs={{0,1},{1,0},{2,3},{3,2},{4,5},{5,4},{6,7},{7,6},{8,9},{9,8},{10,11... | collective-permute-start | bytes 1179656 | tf_op jit(solution)/shard_map/ppermute | solution.py:19
  69.1 19.3 %collective-permute-start.1 = (bf16[2,96,1024]{2,1,0:T(8,128)(2,1)}, bf16[2,96,1024]{2,1,0:T(8,128)(2,1)S(1)}, u32[]{:S(2)}, u32[]{:S(2)}) collective-permute-start(bf16[2,96,1024]{2,1,0:T(8,128)(2,1)} %broadcast_select_fusion.5), channel_id=1, source_target_pairs={{0,1},{1,0},{2,3},{3,2},{4,5},{5,4},{6,7},{7,6},{8,9},{9,8},{10,11... | collective-permute-start | bytes 1179656 | tf_op jit(solution)/shard_map/ppermute | solution.py:19
  70.7 3.1 slice-start.2
  73.4 28.1 %collective-permute-start.3 = (bf16[384,1024]{1,0:T(8,128)(2,1)}, bf16[384,1024]{1,0:T(8,128)(2,1)}, u32[]{:S(2)}, u32[]{:S(2)}) collective-permute-start(bf16[384,1024]{1,0:T(8,128)(2,1)} %fusion.41), channel_id=1, source_target_pairs={{0,1},{1,0},{2,3},{3,2},{4,5},{5,4},{6,7},{7,6},{8,9},{9,8},{10,11... | collective-permute-start | bytes 2359304 | tf_op jit(solution)/shard_map/ppermute | solution.py:19
  105.2 4.1 copy-start.9
  109.3 4.6 copy-start.11
  109.4 2.8 copy-start.8
  111.4 12.3 %copy-start.12 = (bf16[2,96,1024]{2,1,0:T(8,128)(2,1)S(1)}, bf16[2,96,1024]{2,1,0:T(8,128)(2,1)}, u32[]{:S(2)}) copy-start(bf16[2,96,1024]{2,1,0:T(8,128)(2,1)} %add_convert_fusion.5) | copy-start | bytes 1179652
  111.4 12.1 %collective-permute-start.4 = (bf16[2,96,1024]{2,1,0:T(8,128)(2,1)S(1)}, bf16[2,96,1024]{2,1,0:T(8,128)(2,1)S(1)}, u32[]{:S(2)}, u32[]{:S(2)}) collective-permute-start(bf16[2,96,1024]{2,1,0:T(8,128)(2,1)S(1)} %broadcast_select_fusion.3), channel_id=1, source_target_pairs={{0,1},{1,0},{2,3},{3,2},{4,5},{5,4},{6,7},{7,6},{8,9},{9,8},{10,11... | collective-permute-start | bytes 1179656 | tf_op jit(solution)/shard_map/ppermute | solution.py:19
  113.9 32.4 %collective-permute-start.6 = (bf16[384,1024]{1,0:T(8,128)(2,1)S(1)}, bf16[384,1024]{1,0:T(8,128)(2,1)}, u32[]{:S(2)}, u32[]{:S(2)}) collective-permute-start(bf16[384,1024]{1,0:T(8,128)(2,1)S(1)} %fusion.44.after), channel_id=1, source_target_pairs={{0,1},{1,0},{2,3},{3,2},{4,5},{5,4},{6,7},{7,6},{8,9},{9,8},{10,11... | collective-permute-start | bytes 2359304 | tf_op jit(solution)/shard_map/ppermute | solution.py:19
  116.1 28.0 %collective-permute-start.5 = (bf16[2,96,1024]{2,1,0:T(8,128)(2,1)}, bf16[2,96,1024]{2,1,0:T(8,128)(2,1)}, u32[]{:S(2)}, u32[]{:S(2)}) collective-permute-start(bf16[2,96,1024]{2,1,0:T(8,128)(2,1)} %broadcast_select_fusion.2), channel_id=1, source_target_pairs={{0,1},{1,0},{2,3},{3,2},{4,5},{5,4},{6,7},{7,6},{8,9},{9,8},{10,11... | collective-permute-start | bytes 1179656 | tf_op jit(solution)/shard_map/ppermute | solution.py:19
  124.7 23.7 %copy-start.14 = (s32[2]{0:T(128)S(1)}, s32[2]{0:T(128)}, u32[]{:S(2)}) copy-start(s32[2]{0:T(128)} %param.11) | copy-start | bytes 28
  145.4 3.4 copy-start.4
  146.3 2.4 copy-start.5
  148.1 363.3 %all-gather.17.cloned.1.call-start = ((), (), s32[]{:S(2)}) async-start(), calls=%async_computation.7 | async-start | bytes 2359296 | tf_op jit(solution)/shard_map/all_gather | solution.py:231
  148.7 424.1 %reduce-scatter.3.cloned.1.call-start = ((), (), s32[]{:S(2)}) async-start(), calls=%async_computation.2 | async-start | bytes 1966080 | tf_op jit(solution)/shard_map/reduce_scatter | solution.py:270
  148.7 2.3 copy-start
  151.0 2.3 copy-start.2
  170.2 32.2 %copy-start.15 = (bf16[1024,2048]{1,0:T(8,128)(2,1)S(1)}, bf16[1024,2048]{1,0:T(8,128)(2,1)}, u32[]{:S(2)}) copy-start(bf16[1024,2048]{1,0:T(8,128)(2,1)} %param.9) | copy-start | bytes 12582916
  170.2 31.2 %collective-permute-start.8 = (bf16[2,192,1024]{2,1,0:T(8,128)(2,1)S(1)}, bf16[2,192,1024]{2,1,0:T(8,128)(2,1)S(1)}, u32[]{:S(2)}, u32[]{:S(2)}) collective-permute-start(bf16[2,192,1024]{2,1,0:T(8,128)(2,1)S(1)} %get-tuple-element.27), channel_id=1, source_target_pairs={{0,1},{1,0},{2,3},{3,2},{4,5},{5,4},{6,7},{7,6},{8,9},{9,8},{10,11... | collective-permute-start | bytes 2359304 | tf_op jit(solution)/shard_map/ppermute | solution.py:19
  171.1 30.2 %collective-permute-start.7 = (f32[2,192,8]{2,1,0:T(8,128)S(1)}, f32[2,192,8]{2,1,0:T(8,128)S(1)}, u32[]{:S(2)}, u32[]{:S(2)}) collective-permute-start(f32[2,192,8]{2,1,0:T(8,128)S(1)} %bitcast.128), channel_id=1, source_target_pairs={{0,1},{1,0},{2,3},{3,2},{4,5},{5,4},{6,7},{7,6},{8,9},{9,8},{10,11... | collective-permute-start | bytes 36872 | tf_op jit(solution)/shard_map/ppermute | solution.py:19
  205.8 366.9 %reduce-scatter.5.cloned.1.call-start = ((), (), s32[]{:S(2)}) async-start(), calls=%async_computation.3 | async-start | bytes 1966080 | tf_op jit(solution)/shard_map/reduce_scatter | solution.py:270
  206.0 2.3 copy-start.1
  208.2 2.3 copy-start.3
  227.8 275.2 %collective-permute-start.10 = (bf16[2,192,1024]{2,1,0:T(8,128)(2,1)}, bf16[2,192,1024]{2,1,0:T(8,128)(2,1)S(1)}, u32[]{:S(2)}, u32[]{:S(2)}) collective-permute-start(bf16[2,192,1024]{2,1,0:T(8,128)(2,1)} %get-tuple-element.30), channel_id=1, source_target_pairs={{0,1},{1,0},{2,3},{3,2},{4,5},{5,4},{6,7},{7,6},{8,9},{9,8},{10,11... | collective-permute-start | bytes 2359304 | tf_op jit(solution)/shard_map/ppermute | solution.py:19
  230.0 273.0 %collective-permute-start.9 = (f32[2,192,8]{2,1,0:T(8,128)S(1)}, f32[2,192,8]{2,1,0:T(8,128)S(1)}, u32[]{:S(2)}, u32[]{:S(2)}) collective-permute-start(f32[2,192,8]{2,1,0:T(8,128)S(1)} %bitcast.127), channel_id=1, source_target_pairs={{0,1},{1,0},{2,3},{3,2},{4,5},{5,4},{6,7},{7,6},{8,9},{9,8},{10,11... | collective-permute-start | bytes 36872 | tf_op jit(solution)/shard_map/ppermute | solution.py:19
  502.9 2.2 copy-start.16
  568.0 4.8 copy-start.6
Sparse Core Ops, SparseCore 0:
  10.1 39.9 all-gather.10
  51.7 35.9 all-gather.12
  148.2 33.3 all-gather.14
  183.0 30.7 all-gather.16
  215.9 35.2 reduce-scatter.2
  509.8 35.0 reduce-scatter.4

commit v4 on v2

--- a/solution.py
+++ b/solution.py
@@ -160,6 +160,8 @@
     mean = sums[0] / D
     rstd = lax.rsqrt(sums[1] / D - mean * mean + norm_eps)
     stats = lax.all_gather(jnp.stack([mean, rstd]), "gx", axis=0)
+    stats, split_from = lax.optimization_barrier((stats, kv_cache))
+    old_keys, old_values = split_cache(split_from)
 
     depth, local_heads = w_qkv.shape[:2]
     head_size = w_qkv.shape[2] // 3
@@ -188,12 +190,15 @@
             for w in (w_k, w_v)
         ]
         q = jnp.dot(normed, w_q, preferred_element_type=jnp.float32).astype(jnp.bfloat16)
-        if c == 0:
-            q, kv_cache = lax.optimization_barrier((q, kv_cache))
         keys.append(scatter_gy(kv[0]))
         values.append(scatter_gy(kv[1]))
         queries.append(sum_gy(q).reshape(requests, rows, width))
-    old_keys, old_values = split_cache(kv_cache)
+        if c + 1 < CHUNKS:
+            keys, values, queries, old_keys, old_values, gathered[c + 1] = (
+                lax.optimization_barrier(
+                    (keys, values, queries, old_keys, old_values, gathered[c + 1])
+                )
+            )
 
     flat = jnp.arange(rows, dtype=jnp.int32)
     tokens = [(flat // piece) * local_rows + c * piece + flat % piece for c in range(CHUNKS)]
@@ -208,9 +213,7 @@
         full = full.reshape(requests, CHUNKS, share, piece, width).transpose(0, 2, 1, 3, 4)
         return full.reshape(requests, group, width)
 
-    sent_keys, sent_values, queries[-1] = lax.optimization_barrier(
-        (own_keys, own_values, queries[-1])
-    )
+    sent_keys, sent_values, queries = lax.optimization_barrier((own_keys, own_values, queries))
     fresh = jnp.stack([whole(sent_keys), whole(sent_values)], axis=2)
     window = min(group, block)
     padded = jnp.pad(fresh, ((0, 0), (window, window), (0, 0), (0, 0)))

time: 357 us -> 308 us (0.86)
  waiting for transfers between devices: 142 us -> 94.8 us
  local copies, waits for them, and re-layouts: 87.2 us -> 78.8 us
  matrix products: 30.2 us -> 35.4 us
    all_gather x2, waiting for transfers between devices: 51.3 us -> 0.02 us  [shards(): lax.all_gather(hidden[c * piece:(c + 1) * piece], 'gx', axis=0)]
    optimization_barrier x2 -> x1, local copies, waits for them, and re-layouts: 18.5 us -> 8.58 us  [shards(): stats, split_from = lax.optimization_barrier((stats, kv_cache))]
    dynamic_slice x0 -> x1, local copies, waits for them, and re-layouts: none -> 5.73 us  [shards(): old = lax.dynamic_slice_in_dim(kv_cache[r], begin, window)]
    slice x1, local copies, waits for them, and re-layouts: 9.12 us -> 4.7 us  [split_cache(): ordered[:, :, half:].reshape(requests, block, width)]
    unnamed x34 -> x42, local copies, waits for them, and re-layouts: 9.81 us -> 9.34 us
  transfers between devices with their start and end apart: 17 -> 17, of which waited for: 10 -> 8; matrix products, arithmetic and copies ran while one was open for 29% -> 34% of each run, Pallas kernels for 9% -> 11%
where the time goes in v4:
time: 308 us; the launch traced here: 307 us
  waiting for transfers between devices  94.8 us (31%)
  local copies, waits for them, and re-layouts  78.8 us (26%)
  matrix products  35.4 us (11%)
  Pallas kernels  34.5 us (11%)
  other arithmetic  22.5 us (7%)
  between operations  15.8 us (5%)
  starting transfers between devices  12.8 us (4%)
  blocking collectives  12.5 us (4%)
    ppermute x11, waiting for transfers between devices, other(): return lax.ppermute(value, 'gy', [(0, 1), (1, 0)])  79.8 us
    pallas_call x2, Pallas kernels, attend(): pl.pallas_call(functools.partial(attend_kernel, 1.0 / math.sqrt(size)), g...  34.5 us
    reduce_scatter x2, waiting for transfers between devices, shards(): lax.psum_scatter(jnp.dot(attn, w_out, preferred_element_type=jnp.float32)...  14.7 us
    reshape x1, local copies, waits for them, and re-layouts, split_cache(): rows = cache.reshape(requests, 2 * block // size, size, width)  14 us
    ppermute x11, starting transfers between devices, other(): return lax.ppermute(value, 'gy', [(0, 1), (1, 0)])  12.5 us
    all_gather x1, blocking collectives, shards(): stats = lax.all_gather(jnp.stack([mean, rstd]), 'gx', axis=0)  12.5 us
    dot_general x1, matrix products, split_cache(): jnp.einsum('ks,rbsd->rbkd', pick, rows, preferred_element_type=jnp.float32)  10.1 us
    dot_general x4, matrix products, shards(): jnp.dot(normed, w, preferred_element_type=jnp.float32).astype(jnp.bfloat16)  9.65 us
  transfers between devices with their start and end apart: 17, of which 8 were waited for; matrix products, arithmetic and copies ran while one was open for 34% of the time, Pallas kernels for 11%

profile of v4, /device:TPU:0, one launch (start us, length us, event | category | flops | bytes accessed | tf_op | source)
XLA Modules:
  0.0 306.9 jit_solution(5372579982034936689)
XLA Ops:
  7.2 8.6 %copy.95 = bf16[2,1088,2,1024]{3,2,1,0:T(2,128)(2,1)} copy(bf16[2,1088,2,1024]{3,2,1,0:T(2,128)(2,1)} %param.10) | data formatting | bytes 17825792 | tf_op jit(solution)/shard_map/optimization_barrier | solution.py:163
  15.8 0.9 fusion.86
  17.2 3.0 collective-permute-start
  20.3 9.2 %fusion.82 = (bf16[2048,8,128]{2,1,0:T(8,128)(2,1)}, bf16[2048,8,128]{2,1,0:T(8,128)(2,1)}, bf16[2048,8,128]{2,1,0:T(8,128)(2,1)}) fusion(bf16[2048,8,384]{2,1,0:T(8,128)(2,1)} %param.8), kind=kLoop, calls=%fused_computation.133 | loop fusion | bytes 25165824 | tf_op jit(solution)/shard_map/slice | solution.py:169
  29.5 12.5 %all-gather.5 = f32[4,2,192]{2,1,0:T(2,128)S(1)} all-gather(f32[1,2,192]{2,1,0:T(2,128)S(1)} %maximum_bitcast_fusion), channel_id=3, replica_groups=mesh['req'=4,'gx'=4,'gy'=2] {'gx'}, dimensions={0}, use_global_device_ids=true | all-gather | bytes 7680 | tf_op jit(solution)/shard_map/all_gather | solution.py:162
  42.1 14.0 %reshape.222 = bf16[2,17,128,1024]{3,2,1,0:T(8,128)(2,1)} reshape(bf16[2,1088,2,1024]{3,2,1,0:T(2,128)(2,1)} %copy.95) | data formatting | bytes 17825792 | tf_op jit(solution)/shard_map/reshape | solution.py:64
  56.1 10.1 %convert_bitcast_fusion = bf16[2,17,128,1024]{3,2,1,0:T(8,128)(2,1)} fusion(bf16[2,17,128,1024]{3,2,1,0:T(8,128)(2,1)} %reshape.222, s32[128]{0:T(128)S(1)} %fusion.79), kind=kOutput, calls=%fused_computation.6 | convolution fusion | flops 1145323520 | bytes 17826304 | tf_op jit(solution)/shard_map/ks,rbsd->rbkd/dot_general | solution.py:69
  66.2 1.9 fusion.24
  68.1 4.1 %fusion.31 = bf16[384,1024]{1,0:T(8,128)(2,1)S(1)} fusion(bf16[384,2048]{1,0:T(8,128)(2,1)S(1)} %bitcast.154, bf16[256,8,8,128]{3,2,1,0:T(8,128)(2,1)} %bitcast.138), kind=kOutput, calls=%fused_computation.51 | convolution fusion | flops 1611005952 | bytes 6553600 | tf_op jit(solution)/shard_map/dot_general | solution.py:187
  72.3 1.8 fusion.37
  74.2 0.6 collective-permute-start.2
  74.8 0.8 broadcast_select_fusion.3
  75.6 1.5 collective-permute-start.1
  77.1 2.7 fusion.43
  79.7 0.5 collective-permute-start.3
  80.3 4.7 %fusion.85 = (bf16[2,17,64,1024]{3,2,1,0:T(8,128)(2,1)}, bf16[2,17,64,1024]{3,2,1,0:T(8,128)(2,1)}) fusion(bf16[2,17,128,1024]{3,2,1,0:T(8,128)(2,1)S(1)} %bitcast.133), kind=kLoop, calls=%fused_computation.136 | loop fusion | bytes 17825792 | tf_op jit(solution)/shard_map/slice | solution.py:73
  85.0 1.4 collective-permute-done.2
  86.4 1.2 add_convert_fusion.4
  87.6 7.1 %collective-permute-done.1 = bf16[2,96,1024]{2,1,0:T(8,128)(2,1)S(1)} collective-permute-done((bf16[2,96,1024]{2,1,0:T(8,128)(2,1)}, bf16[2,96,1024]{2,1,0:T(8,128)(2,1)S(1)}, u32[]{:S(2)}, u32[]{:S(2)}) %collective-permute-start.1) | collective-permute-done | bytes 393248 | tf_op jit(solution)/shard_map/ppermute | solution.py:19
  94.9 13.0 %collective-permute-done.3 = bf16[384,1024]{1,0:T(8,128)(2,1)} collective-permute-done((bf16[384,1024]{1,0:T(8,128)(2,1)}, bf16[384,1024]{1,0:T(8,128)(2,1)}, u32[]{:S(2)}, u32[]{:S(2)}) %collective-permute-start.3) | collective-permute-done | bytes 786464 | tf_op jit(solution)/shard_map/ppermute | solution.py:19
  107.9 1.7 add_convert_fusion.1
  109.6 1.9 multiply_convert_fusion
  111.6 5.0 %fusion.46 = bf16[384,1024]{1,0:T(8,128)(2,1)} fusion(bf16[384,2048]{1,0:T(8,128)(2,1)S(1)} %bitcast.157, bf16[256,8,8,128]{3,2,1,0:T(8,128)(2,1)} %bitcast.140), kind=kOutput, calls=%fused_computation.56 | convolution fusion | flops 1611005952 | bytes 6553600 | tf_op jit(solution)/shard_map/dot_general | solution.py:192
  116.6 2.0 fusion.34
  118.6 0.6 collective-permute-start.4
  119.3 1.8 fusion.40
  121.0 1.5 collective-permute-start.6
  122.6 0.8 broadcast_select_fusion
  123.4 0.6 collective-permute-start.5
  124.0 6.8 %collective-permute-done.4 = bf16[2,96,1024]{2,1,0:T(8,128)(2,1)S(1)} collective-permute-done((bf16[2,96,1024]{2,1,0:T(8,128)(2,1)S(1)}, bf16[2,96,1024]{2,1,0:T(8,128)(2,1)S(1)}, u32[]{:S(2)}, u32[]{:S(2)}) %collective-permute-start.4) | collective-permute-done | bytes 393248 | tf_op jit(solution)/shard_map/ppermute | solution.py:19
  130.9 0.9 pad_maximum_fusion.nk_ref
  131.9 19.5 %collective-permute-done.5 = bf16[2,96,1024]{2,1,0:T(8,128)(2,1)S(1)} collective-permute-done((bf16[2,96,1024]{2,1,0:T(8,128)(2,1)}, bf16[2,96,1024]{2,1,0:T(8,128)(2,1)S(1)}, u32[]{:S(2)}, u32[]{:S(2)}) %collective-permute-start.5) | collective-permute-done | bytes 393248 | tf_op jit(solution)/shard_map/ppermute | solution.py:19
  151.6 0.9 pad_maximum_fusion.1.nv_ref
  152.5 1.7 add_convert_fusion
  154.9 2.3 copy-done
  157.2 2.3 copy-done.2
  159.5 16.9 %shard_map.77 = (bf16[2,192,1024]{2,1,0:T(8,128)(2,1)S(1)}, f32[2,192,128]{2,1,0:T(8,128)S(1)}) custom-call(s32[3]{0:T(128)S(1)} %pad_add_fusion.1.info, f32[8]{0:T(128)S(1)} %multiply_exponential_fusion.slopes, bf16[2,192,1024]{2,1,0:T(8,128)(2,1)S(1)} %bitcast.125, bf16[2,1088,1024]{2,1,0:T(8,128)(2,1)S(1)} %bitcast.123, ...), custom_call_target="tpu_custom_call" | custom-call | flops 2013265920 | bytes 12058624 | tf_op jit(solution)/shard_map/pallas_call | solution.py:119
  176.4 0.7 collective-permute-start.8
  177.0 1.4 collective-permute-start.7
  178.5 28.1 %collective-permute-done.7 = f32[2,192,8]{2,1,0:T(8,128)S(1)} collective-permute-done((f32[2,192,8]{2,1,0:T(8,128)S(1)}, f32[2,192,8]{2,1,0:T(8,128)S(1)}, u32[]{:S(2)}, u32[]{:S(2)}) %collective-permute-start.7) | collective-permute-done | bytes 12320 | tf_op jit(solution)/shard_map/ppermute | solution.py:19
  206.7 0.5 mul.148
  207.1 0.5 mul.151
  207.6 3.4 %convolution_convert_fusion.1 = bf16[384,2048]{1,0:T(8,128)(2,1)} fusion(bf16[1024,2048]{1,0:T(8,128)(2,1)S(1)} %copy-done.16, f32[48,8,8,128]{3,2,1,0:T(8,128)S(1)} %bitcast.162, f32[48,8,8,128]{3,2,1,0:T(8,128)S(1)} %bitcast.160, bf16[384,1024]{1,0:T(8,128)(2,1)S(1)} %bitcast.173, bf16[384,1024]{1,0:T(8,128)(2,1)S(1)} %bitcast.131), kind=kOutput, calls=%fused_computation.31 | convolution fusion | flops 1613758464 | bytes 10485760 | tf_op jit(solution)/shard_map/dot_general | solution.py:252
  211.2 2.3 copy-done.1
  213.4 2.3 copy-done.3
  215.7 17.6 %shard_map.78 = (bf16[2,192,1024]{2,1,0:T(8,128)(2,1)}, f32[2,192,128]{2,1,0:T(8,128)S(1)}) custom-call(s32[3]{0:T(128)S(1)} %pad_add_fusion.1.info, f32[8]{0:T(128)S(1)} %multiply_exponential_fusion.slopes, bf16[2,192,1024]{2,1,0:T(8,128)(2,1)S(1)} %bitcast.126, bf16[2,1088,1024]{2,1,0:T(8,128)(2,1)S(1)} %bitcast.124, bf16[2,1088,1024]{2,1,0:T(8,128)(2,1)S(1)} %bitcast.122, ...), custom_call_target="tpu_custom_call" | custom-call | flops 2013265920 | bytes 12058624 | tf_op jit(solution)/shard_map/pallas_call | solution.py:119
  233.6 8.9 %fusion.84 = (bf16[1,1088,2,1024]{3,2,1,0:T(2,128)(2,1)}, bf16[1,1088,2,1024]{3,2,1,0:T(2,128)(2,1)}) fusion(bf16[2,1088,2,1024]{3,2,1,0:T(2,128)(2,1)} %copy.95), kind=kLoop, calls=%fused_computation.135 | loop fusion | bytes 17825792 | tf_op jit(solution)/shard_map/slice | solution.py:229
  242.5 0.7 fusion.88
  244.4 5.7 %constant_dynamic-slice_fusion = (bf16[1,384,2,1024]{3,2,1,0:T(2,128)(2,1)}, bf16[1,384,2,1024]{3,2,1,0:T(2,128)(2,1)}) fusion(bf16[1,1088,2,1024]{3,2,1,0:T(2,128)(2,1)} %get-tuple-element.41, s32[]{:T(128)S(6)} %min.15, bf16[1,1088,2,1024]{3,2,1,0:T(2,128)(2,1)} %get-tuple-element.42, s32[]{:T(128)S(6)} %min.13), kind=kLoop, calls=%fused_computation.115 | loop fusion | bytes 6291464 | tf_op jit(solution)/shard_map/dynamic_slice | solution.py:229
  250.2 1.7 collective-permute-start.9
  251.9 3.9 %collective-permute-done.9 = f32[2,192,8]{2,1,0:T(8,128)S(1)} collective-permute-done((f32[2,192,8]{2,1,0:T(8,128)S(1)}, f32[2,192,8]{2,1,0:T(8,128)S(1)}, u32[]{:S(2)}, u32[]{:S(2)}) %collective-permute-start.9) | collective-permute-done | bytes 12320 | tf_op jit(solution)/shard_map/ppermute | solution.py:19
  255.9 0.5 mul.154
  256.4 0.5 mul.157
  256.9 4.6 %convolution_convert_fusion = bf16[384,2048]{1,0:T(8,128)(2,1)} fusion(bf16[1024,2048]{1,0:T(8,128)(2,1)S(1)} %copy-done.17, f32[48,8,8,128]{3,2,1,0:T(8,128)S(1)} %bitcast.163, f32[48,8,8,128]{3,2,1,0:T(8,128)S(1)} %bitcast.161, bf16[384,1024]{1,0:T(8,128)(2,1)S(1)} %bitcast.172, bf16[384,1024]{1,0:T(8,128)(2,1)} %bitcast.40), kind=kOutput, calls=%fused_computation.30 | convolution fusion | flops 1613758464 | bytes 10485760 | tf_op jit(solution)/shard_map/dot_general | solution.py:252
  261.5 2.7 copy.26
  264.2 1.6 copy.27
  266.1 1.5 fusion.3
  267.6 4.8 %fusion.83 = (bf16[1,1152,2,1024]{3,1,0,2:T(8,128)(2,1)}, bf16[1,1152,2,1024]{3,1,0,2:T(8,128)(2,1)}) fusion(bf16[2,1152,2,1024]{3,1,0,2:T(8,128)(2,1)S(1)} %fusion.3), kind=kLoop, calls=%fused_computation.134 | loop fusion | bytes 18874368 | tf_op jit(solution)/shard_map/slice | solution.py:225
  272.4 2.8 copy_select_fusion.1
  275.3 2.3 copy_select_fusion
  277.6 2.8 copy_dynamic-update-slice_fusion.1
  280.3 2.8 copy_dynamic-update-slice_fusion
  283.1 14.7 %reduce-scatter.5.cloned.1.call-done = bf16[96,2048]{1,0:T(8,128)(2,1)} async-done(((bf16[384,2048]{1,0:T(8,128)(2,1)}), bf16[96,2048]{1,0:T(8,128)(2,1)}) %reduce-scatter.5.cloned.1.call-update) | async-done | bytes 393232 | tf_op jit(solution)/shard_map/reduce_scatter | solution.py:251
  297.8 2.3 fusion.26
  (84 shorter events, 2.9 us)
Async XLA Ops:
  7.2 8.6 %copy-start.6 = (bf16[192,2048]{1,0:T(8,128)(2,1)S(1)}, bf16[192,2048]{1,0:T(8,128)(2,1)}, u32[]{:S(2)}) copy-start(bf16[192,2048]{1,0:T(8,128)(2,1)} %param.6) | copy-start | bytes 2359300
  7.2 59.0 %all-gather.11.cloned.1.call-start = ((), (), s32[]{:S(2)}) async-start(), calls=%async_computation.4 | async-start | bytes 1966080 | tf_op jit(solution)/shard_map/all_gather | solution.py:157
  16.8 92.9 %all-gather.13.cloned.1.call-start = ((), (), s32[]{:S(2)}) async-start(), calls=%async_computation.5 | async-start | bytes 1966080 | tf_op jit(solution)/shard_map/all_gather | solution.py:157
  17.2 12.3 %collective-permute-start = (f32[2,192]{1,0:T(2,128)S(1)}, f32[2,192]{1,0:T(2,128)S(1)}, u32[]{:S(2)}, u32[]{:S(2)}) collective-permute-start(f32[2,192]{1,0:T(2,128)S(1)} %pad_maximum_fusion.2), channel_id=1, source_target_pairs={{0,1},{1,0},{2,3},{3,2},{4,5},{5,4},{6,7},{7,6},{8,9},{9,8},{10,11... | collective-permute-start | bytes 4616 | tf_op jit(solution)/shard_map/ppermute | solution.py:19
  20.3 241.2 %all-gather.15.cloned.1.call-start = ((), (), s32[]{:S(2)}) async-start(), calls=%async_computation.6 | async-start | bytes 2359296 | tf_op jit(solution)/shard_map/all_gather | solution.py:211
  56.1 10.1 %copy-start.14 = (f32[2048]{0:T(1024)S(1)}, f32[2048]{0:T(1024)}, u32[]{:S(2)}) copy-start(f32[2048]{0:T(1024)} %param.7) | copy-start | bytes 24580
  68.1 4.1 %copy-start.10 = (bf16[2048,8,128]{2,1,0:T(8,128)(2,1)S(1)}, bf16[2048,8,128]{2,1,0:T(8,128)(2,1)}, u32[]{:S(2)}) copy-start(bf16[2048,8,128]{2,1,0:T(8,128)(2,1)} %get-tuple-element.38) | copy-start | bytes 12582916
  72.3 4.8 %copy-start.13 = (bf16[2048,8,128]{2,1,0:T(8,128)(2,1)S(1)}, bf16[2048,8,128]{2,1,0:T(8,128)(2,1)}, u32[]{:S(2)}) copy-start(bf16[2048,8,128]{2,1,0:T(8,128)(2,1)} %get-tuple-element.36) | copy-start | bytes 12582916
  72.3 8.0 %slice-start = ((s8[8912896]{0:T(1024)(128)(4,1)}), s8[4194304]{0:T(1024)(128)(4,1)S(1)}, s32[]{:S(2)}) async-start(s8[8912896]{0:T(1024)(128)(4,1)} %bitcast.132), calls=%async_computation.8 | async-start | bytes 8388608
  72.3 8.0 %slice-start.1 = ((s8[8912896]{0:T(1024)(128)(4,1)}), s8[4194304]{0:T(1024)(128)(4,1)S(1)}, s32[]{:S(2)}) async-start(s8[8912896]{0:T(1024)(128)(4,1)} %bitcast.132), calls=%async_computation.9 | async-start | bytes 8388608
  74.2 12.2 %collective-permute-start.2 = (bf16[2,96,1024]{2,1,0:T(8,128)(2,1)S(1)}, bf16[2,96,1024]{2,1,0:T(8,128)(2,1)}, u32[]{:S(2)}, u32[]{:S(2)}) collective-permute-start(bf16[2,96,1024]{2,1,0:T(8,128)(2,1)S(1)} %broadcast_select_fusion.2), channel_id=1, source_target_pairs={{0,1},{1,0},{2,3},{3,2},{4,5},{5,4},{6,7},{7,6},{8,9},{9,8},{10,11... | collective-permute-start | bytes 1179656 | tf_op jit(solution)/shard_map/ppermute | solution.py:19
  75.6 19.1 %collective-permute-start.1 = (bf16[2,96,1024]{2,1,0:T(8,128)(2,1)}, bf16[2,96,1024]{2,1,0:T(8,128)(2,1)S(1)}, u32[]{:S(2)}, u32[]{:S(2)}) collective-permute-start(bf16[2,96,1024]{2,1,0:T(8,128)(2,1)} %broadcast_select_fusion.3), channel_id=1, source_target_pairs={{0,1},{1,0},{2,3},{3,2},{4,5},{5,4},{6,7},{7,6},{8,9},{9,8},{10,11... | collective-permute-start | bytes 1179656 | tf_op jit(solution)/shard_map/ppermute | solution.py:19
  77.1 3.2 %slice-start.2 = ((s8[8912896]{0:T(1024)(128)(4,1)}), s8[524288]{0:T(1024)(128)(4,1)S(1)}, s32[]{:S(2)}) async-start(s8[8912896]{0:T(1024)(128)(4,1)} %bitcast.132), calls=%async_computation.10 | async-start | bytes 1048576
  79.7 28.2 %collective-permute-start.3 = (bf16[384,1024]{1,0:T(8,128)(2,1)}, bf16[384,1024]{1,0:T(8,128)(2,1)}, u32[]{:S(2)}, u32[]{:S(2)}) collective-permute-start(bf16[384,1024]{1,0:T(8,128)(2,1)} %fusion.43), channel_id=1, source_target_pairs={{0,1},{1,0},{2,3},{3,2},{4,5},{5,4},{6,7},{7,6},{8,9},{9,8},{10,11... | collective-permute-start | bytes 2359304 | tf_op jit(solution)/shard_map/ppermute | solution.py:19
  111.6 5.0 %copy-start.12 = (bf16[2048,8,128]{2,1,0:T(8,128)(2,1)S(1)}, bf16[2048,8,128]{2,1,0:T(8,128)(2,1)}, u32[]{:S(2)}) copy-start(bf16[2048,8,128]{2,1,0:T(8,128)(2,1)} %get-tuple-element.37) | copy-start | bytes 12582916
  116.6 2.7 copy-start.11
  118.6 12.1 %collective-permute-start.4 = (bf16[2,96,1024]{2,1,0:T(8,128)(2,1)S(1)}, bf16[2,96,1024]{2,1,0:T(8,128)(2,1)S(1)}, u32[]{:S(2)}, u32[]{:S(2)}) collective-permute-start(bf16[2,96,1024]{2,1,0:T(8,128)(2,1)S(1)} %broadcast_select_fusion.1), channel_id=1, source_target_pairs={{0,1},{1,0},{2,3},{3,2},{4,5},{5,4},{6,7},{7,6},{8,9},{9,8},{10,11... | collective-permute-start | bytes 1179656 | tf_op jit(solution)/shard_map/ppermute | solution.py:19
  121.0 31.5 %collective-permute-start.6 = (bf16[384,1024]{1,0:T(8,128)(2,1)}, bf16[384,1024]{1,0:T(8,128)(2,1)}, u32[]{:S(2)}, u32[]{:S(2)}) collective-permute-start(bf16[384,1024]{1,0:T(8,128)(2,1)} %fusion.46), channel_id=1, source_target_pairs={{0,1},{1,0},{2,3},{3,2},{4,5},{5,4},{6,7},{7,6},{8,9},{9,8},{10,11... | collective-permute-start | bytes 2359304 | tf_op jit(solution)/shard_map/ppermute | solution.py:19
  123.4 28.0 %collective-permute-start.5 = (bf16[2,96,1024]{2,1,0:T(8,128)(2,1)}, bf16[2,96,1024]{2,1,0:T(8,128)(2,1)S(1)}, u32[]{:S(2)}, u32[]{:S(2)}) collective-permute-start(bf16[2,96,1024]{2,1,0:T(8,128)(2,1)} %broadcast_select_fusion), channel_id=1, source_target_pairs={{0,1},{1,0},{2,3},{3,2},{4,5},{5,4},{6,7},{7,6},{8,9},{9,8},{10,11... | collective-permute-start | bytes 1179656 | tf_op jit(solution)/shard_map/ppermute | solution.py:19
  131.9 22.7 %copy-start.15 = (s32[2]{0:T(128)S(1)}, s32[2]{0:T(128)}, u32[]{:S(2)}) copy-start(s32[2]{0:T(128)} %param.11) | copy-start | bytes 28
  151.5 3.4 %copy-start.4 = (bf16[2,192,1024]{2,1,0:T(8,128)(2,1)S(1)}, bf16[2,192,1024]{2,1,0:T(8,128)(2,1)}, u32[]{:S(2)}) copy-start(bf16[2,192,1024]{2,1,0:T(8,128)(2,1)} %pad_maximum_fusion.nk_ref) | copy-start | bytes 2359300
  152.5 2.4 copy-start.5
  154.3 109.9 %all-gather.17.cloned.1.call-start = ((), (), s32[]{:S(2)}) async-start(), calls=%async_computation.7 | async-start | bytes 2359296 | tf_op jit(solution)/shard_map/all_gather | solution.py:211
  154.9 128.2 %reduce-scatter.3.cloned.1.call-start = ((), (), s32[]{:S(2)}) async-start(), calls=%async_computation.2 | async-start | bytes 1966080 | tf_op jit(solution)/shard_map/reduce_scatter | solution.py:251
  154.9 2.3 copy-start
  157.2 2.3 copy-start.2
  176.4 31.3 %copy-start.16 = (bf16[1024,2048]{1,0:T(8,128)(2,1)S(1)}, bf16[1024,2048]{1,0:T(8,128)(2,1)}, u32[]{:S(2)}) copy-start(bf16[1024,2048]{1,0:T(8,128)(2,1)} %param.9) | copy-start | bytes 12582916
  176.4 30.3 %collective-permute-start.8 = (bf16[2,192,1024]{2,1,0:T(8,128)(2,1)S(1)}, bf16[2,192,1024]{2,1,0:T(8,128)(2,1)S(1)}, u32[]{:S(2)}, u32[]{:S(2)}) collective-permute-start(bf16[2,192,1024]{2,1,0:T(8,128)(2,1)S(1)} %get-tuple-element.27), channel_id=1, source_target_pairs={{0,1},{1,0},{2,3},{3,2},{4,5},{5,4},{6,7},{7,6},{8,9},{9,8},{10,11... | collective-permute-start | bytes 2359304 | tf_op jit(solution)/shard_map/ppermute | solution.py:19
  177.0 29.5 %collective-permute-start.7 = (f32[2,192,8]{2,1,0:T(8,128)S(1)}, f32[2,192,8]{2,1,0:T(8,128)S(1)}, u32[]{:S(2)}, u32[]{:S(2)}) collective-permute-start(f32[2,192,8]{2,1,0:T(8,128)S(1)} %bitcast.128), channel_id=1, source_target_pairs={{0,1},{1,0},{2,3},{3,2},{4,5},{5,4},{6,7},{7,6},{8,9},{9,8},{10,11... | collective-permute-start | bytes 36872 | tf_op jit(solution)/shard_map/ppermute | solution.py:19
  211.1 86.8 %reduce-scatter.5.cloned.1.call-start = ((), (), s32[]{:S(2)}) async-start(), calls=%async_computation.3 | async-start | bytes 1966080 | tf_op jit(solution)/shard_map/reduce_scatter | solution.py:251
  211.2 2.3 copy-start.1
  213.4 2.3 copy-start.3
  233.3 22.7 %collective-permute-start.10 = (bf16[2,192,1024]{2,1,0:T(8,128)(2,1)}, bf16[2,192,1024]{2,1,0:T(8,128)(2,1)S(1)}, u32[]{:S(2)}, u32[]{:S(2)}) collective-permute-start(bf16[2,192,1024]{2,1,0:T(8,128)(2,1)} %get-tuple-element.30), channel_id=1, source_target_pairs={{0,1},{1,0},{2,3},{3,2},{4,5},{5,4},{6,7},{7,6},{8,9},{9,8},{10,11... | collective-permute-start | bytes 2359304 | tf_op jit(solution)/shard_map/ppermute | solution.py:19
  250.2 5.7 %collective-permute-start.9 = (f32[2,192,8]{2,1,0:T(8,128)S(1)}, f32[2,192,8]{2,1,0:T(8,128)S(1)}, u32[]{:S(2)}, u32[]{:S(2)}) collective-permute-start(f32[2,192,8]{2,1,0:T(8,128)S(1)} %bitcast.127), channel_id=1, source_target_pairs={{0,1},{1,0},{2,3},{3,2},{4,5},{5,4},{6,7},{7,6},{8,9},{9,8},{10,11... | collective-permute-start | bytes 36872 | tf_op jit(solution)/shard_map/ppermute | solution.py:19
  251.9 5.0 %copy-start.17 = (bf16[1024,2048]{1,0:T(8,128)(2,1)S(1)}, bf16[1024,2048]{1,0:T(8,128)(2,1)}, u32[]{:S(2)}) copy-start(bf16[1024,2048]{1,0:T(8,128)(2,1)} %param.9) | copy-start | bytes 12582916
  264.2 1.9 copy-start.8
  272.4 2.9 copy-start.9
  277.6 20.3 %copy-start.7 = (bf16[192,2048]{1,0:T(8,128)(2,1)S(1)}, bf16[192,2048]{1,0:T(8,128)(2,1)}, u32[]{:S(2)}) copy-start(bf16[192,2048]{1,0:T(8,128)(2,1)} %param.6) | copy-start | bytes 2359300
Sparse Core Ops, SparseCore 0:
  16.9 39.9 all-gather.10
  58.4 35.9 all-gather.12
  154.4 33.1 all-gather.14
  189.0 30.8 all-gather.16
  222.1 35.3 reduce-scatter.2
  261.6 36.1 reduce-scatter.4
